TPU v7x, 512 devices: a whole 4x4x16 slice. The times are simulated.
512 devices in a mesh: grp: 16 (over z), dev: 32 (over x, y, core).
Axes of the slice: x: 4, y: 4, z: 16, core: 2. Of those that a mesh axis runs over, the one named last changes fastest.
Arguments:
- proj: bfloat16 [65536, 4096], P(('grp', 'dev')), may hold values from -6 to 6
- resid: bfloat16 [65536, 1024], P(('grp', 'dev')), may hold values from -6 to 6
- send_rows: int32 [512, 256], P(('grp', 'dev')), may hold values from 0 to 128, as said below
- pack_rows: int32 [512, 128], P(('grp', 'dev')), may hold values from 0 to 255, as said below
- segments: int32 [512, 128], P(('grp', 'dev')), may hold values from 0 to 3, never falling along the last dimension, each value on 1 to 64 neighbouring positions
- targets: int32 [512, 128], P(('grp', 'dev')), may hold values from 0 to 511
- ratios: float32 [512, 128], P(('grp', 'dev')), may hold values from 0.1 to 40
- negatives: int32 [16, 256], P('grp'), may hold values from 0 to 511
- table: bfloat16 [8192, 1024], P(('grp', 'dev')), may hold values from -6 to 6
- out_weight: bfloat16 [1024, 1024], P('dev'), may hold values from -0.1875 to 0.1875
- topk: int32 [1], replicated, may hold values from 2 to 16
Outputs:
- loss: float32 [1], replicated
- d_proj: bfloat16 [65536, 4096], P(('grp', 'dev'))
- d_table: float32 [8192, 1024], P(('grp', 'dev'))
Inputs may be any that keep to these rules, and one draw needn't show every extreme that they name: `send_rows`: A device's slots name, for each of its 32 peers in turn, 8 slots holding distinct arrival rows of that device sent to that peer, then 128 in each unused slot; every arrival row is sent exactly once and every device receives 128 rows; in every group some device fills all 8 slots to one peer. `pack_rows`: each device's packed rows name distinct used received slots, numbered source member times 8 plus the place in that source's slots.
All inputs are finite; a program needn't handle non-finite values.
Results may differ from a plain program's by a relative error of at most 0.022.
Values may be sent and summed in bfloat16 or wider, within the bound.
No kernel may reach another device: no remote copies, remote signals or barrier semaphores. Data moves between devices by JAX's collectives and lax.ppermute only.
A program may use at most 64 MiB of HBM per device.

v0:
```python
import jax
import jax.numpy as jnp
from jax import lax
from jax.sharding import PartitionSpec as P

HEADS = 8


sharpness = 20.0


def silu_grad(values):
    logistic = jax.nn.sigmoid(values)
    return logistic * (1.0 + values * (1.0 - logistic))


def shards(
    proj, resid, send_rows, pack_rows, segments, targets, ratios, negatives, table, out_weight, topk
):
    row_count = proj.shape[0]
    model_width = resid.shape[1]
    slot_rows = send_rows[0]
    occupied = (slot_rows < row_count)[:, None]
    clipped = jnp.minimum(slot_rows, row_count - 1)
    send_proj = jnp.where(occupied, jnp.take(proj, clipped, axis=0), jnp.zeros((), proj.dtype))
    send_resid = jnp.where(occupied, jnp.take(resid, clipped, axis=0), jnp.zeros((), resid.dtype))
    total_ratio = lax.psum(jnp.sum(ratios), ("grp", "dev"))
    got_proj, got_resid = (
        lax.all_to_all(send_proj, "dev", split_axis=0, concat_axis=0, tiled=True),
        lax.all_to_all(send_resid, "dev", split_axis=0, concat_axis=0, tiled=True),
    )
    pack_order = pack_rows[0]
    segment = segments[0]
    pre_act = jnp.take(got_proj, pack_order, axis=0).astype(jnp.float32)
    activated = jax.nn.silu(pre_act)
    act_bf = activated.astype(jnp.bfloat16)
    gate_u = activated[:, :model_width]
    value_h = act_bf[:, model_width : 2 * model_width].reshape(row_count, HEADS, -1)
    query_h = act_bf[:, 2 * model_width : 3 * model_width].reshape(row_count, HEADS, -1)
    key_h = act_bf[:, 3 * model_width :].reshape(row_count, HEADS, -1)
    head_dim = value_h.shape[2]
    scaling = head_dim ** (-0.5)
    norm_len = row_count // 2
    positions = jnp.arange(row_count)
    causal_mask = (segment[:, None] == segment[None, :]) & (
        positions[None, :] <= positions[:, None]
    )
    scores = (
        jnp.einsum("ihd,jhd->hij", query_h, key_h, preferred_element_type=jnp.float32) * scaling
    )
    att_bf = (jnp.where(causal_mask[None], jax.nn.silu(scores), 0.0) / norm_len).astype(
        jnp.bfloat16
    )
    mixed = jnp.einsum("hij,jhd->ihd", att_bf, value_h, preferred_element_type=jnp.float32).reshape(
        row_count, model_width
    )
    row_mean = jnp.mean(mixed, 1, keepdims=True)
    centered = mixed - row_mean
    inv_dev = lax.rsqrt(jnp.mean(centered * centered, 1, keepdims=True) + 1e-05)
    normed = centered * inv_dev
    gated_bf = (normed * gate_u).astype(jnp.bfloat16)
    resid_rows = jnp.take(got_resid, pack_order, axis=0).astype(jnp.float32)
    weight_full = lax.all_gather(out_weight, "dev", axis=0, tiled=True)
    output = resid_rows + jnp.dot(gated_bf, weight_full, preferred_element_type=jnp.float32)
    inv_out = lax.rsqrt(jnp.sum(output * output, 1, keepdims=True) + 1e-06)
    user = output * inv_out
    user_bf = user.astype(jnp.bfloat16)
    gathered = lax.all_gather(table, "dev", axis=0, tiled=True)
    tab_rows = gathered.astype(jnp.float32)
    item_bf = (tab_rows * lax.rsqrt(jnp.sum(tab_rows * tab_rows, 1, keepdims=True) + 1e-06)).astype(
        jnp.bfloat16
    )
    logits = sharpness * jnp.einsum(
        "td,md->tm", user_bf, item_bf, preferred_element_type=jnp.float32
    )
    item_ids = jnp.arange(logits.shape[1])
    onehot = (targets[0][:, None] == item_ids[None, :]).astype(jnp.float32)
    counts = jnp.sum((negatives[0][:, None] == item_ids[None, :]).astype(jnp.float32), 0)
    weighted = counts[None, :] + onehot
    exponent = jnp.exp(logits)
    totals = jnp.sum(weighted * exponent, 1)
    positive = jnp.sum(onehot * logits, 1)
    target_prob = jnp.exp(positive) / totals
    row_loss = jnp.log(totals) - positive
    topk_value = topk[0].astype(jnp.float32)
    correction = topk_value * jnp.power(1.0 - target_prob, topk_value - 1.0)
    row_weight = ratios[0] * correction
    numerator = jnp.sum(row_weight * row_loss)
    row_coef = row_weight / total_ratio
    d_logits = row_coef[:, None] * (weighted * exponent / totals[:, None] - onehot)
    grad_bf = (sharpness * d_logits).astype(jnp.bfloat16)
    d_user = jnp.dot(grad_bf, item_bf, preferred_element_type=jnp.float32)
    d_item = jnp.einsum("tm,td->md", grad_bf, user_bf, preferred_element_type=jnp.float32)
    summed = lax.psum_scatter(
        d_item.astype(jnp.bfloat16), "dev", scatter_dimension=0, tiled=True
    ).astype(jnp.float32)
    own_rows = table.astype(jnp.float32)
    inv_own = lax.rsqrt(jnp.sum(own_rows * own_rows, 1, keepdims=True) + 1e-06)
    own_item = own_rows * inv_own
    d_table = inv_own * (summed - own_item * jnp.sum(own_item * summed, 1, keepdims=True))
    d_output = inv_out * (d_user - user * jnp.sum(user * d_user, 1, keepdims=True))
    dout_bf = d_output.astype(jnp.bfloat16)
    d_gated = jnp.einsum("te,de->td", dout_bf, weight_full, preferred_element_type=jnp.float32)
    d_normed = d_gated * gate_u
    d_gate = d_gated * normed
    d_mixed = inv_dev * (
        d_normed
        - jnp.mean(d_normed, 1, keepdims=True)
        - normed * jnp.mean(d_normed * normed, 1, keepdims=True)
    )
    dmix_bf = d_mixed.astype(jnp.bfloat16).reshape(row_count, HEADS, -1)
    d_att = jnp.einsum("ihd,jhd->hij", dmix_bf, value_h, preferred_element_type=jnp.float32)
    d_value = jnp.einsum("hij,ihd->jhd", att_bf, dmix_bf, preferred_element_type=jnp.float32)
    d_scores = (
        jnp.where(causal_mask[None], d_att * silu_grad(scores), 0.0) * (scaling / norm_len)
    ).astype(jnp.bfloat16)
    d_query = jnp.einsum("hij,jhd->ihd", d_scores, key_h, preferred_element_type=jnp.float32)
    d_key = jnp.einsum("hij,ihd->jhd", d_scores, query_h, preferred_element_type=jnp.float32)
    d_act = jnp.concatenate(
        [
            d_gate,
            d_value.reshape(row_count, model_width),
            d_query.reshape(row_count, model_width),
            d_key.reshape(row_count, model_width),
        ],
        1,
    )
    d_proj = (d_act * silu_grad(pre_act)).astype(jnp.bfloat16)
    loss_sum = lax.psum(numerator, ("grp", "dev"))
    loss = (loss_sum / total_ratio).reshape(1)
    return (loss, d_proj, d_table)


def solution(mesh):
    return jax.shard_map(
        shards,
        mesh=mesh,
        in_specs=(
            P(("grp", "dev"), None),
            P(("grp", "dev"), None),
            P(("grp", "dev"), None),
            P(("grp", "dev"), None),
            P(("grp", "dev"), None),
            P(("grp", "dev"), None),
            P(("grp", "dev"), None),
            P("grp", None),
            P(("grp", "dev"), None),
            P("dev", None),
            P(),
        ),
        out_specs=(P(), P(("grp", "dev"), None), P(("grp", "dev"), None)),
        check_vma=False,
    )
```

profile of v0, /device:TPU:1, one launch (start us, length us, event | category | flops | bytes accessed | tf_op | source)
XLA Modules:
  0.0 364.7 jit_solution(12245560360310896795)
XLA Ops:
  7.2 0.0 all-gather.5.cloned.1.call-start
  7.2 0.7 all-gather.5.cloned.1.call-update
  7.9 0.7 compare_select_fusion.1
  8.6 0.7 minimum_reduce_fusion
  9.3 0.7 compare_reduce_fusion
  10.0 0.1 min.26
  10.1 0.1 lt.72
  10.2 2.5 gather_fusion
  12.8 0.9 fusion.15
  13.7 10.4 %all-to-all-start = ((bf16[32,8,1024]{2,1,0:T(8,128)(2,1)}), bf16[32,8,1024]{2,1,0:T(8,128)(2,1)S(1)}, u32[]{:S(2)}, u32[]{:S(2)}) async-start(bf16[32,8,1024]{2,1,0:T(8,128)(2,1)} %fusion.15), calls=%async_computation | async-start | bytes 1048576 | tf_op jit(solution)/shard_map/all_to_all | solution.py:30
  24.1 3.2 gather_fusion.2
  27.3 3.2 fusion.9
  30.6 5.3 %all-to-all-done = bf16[32,8,1024]{2,1,0:T(8,128)(2,1)S(1)} async-done(((bf16[32,8,1024]{2,1,0:T(8,128)(2,1)}), bf16[32,8,1024]{2,1,0:T(8,128)(2,1)S(1)}, u32[]{:S(2)}, u32[]{:S(2)}) %all-to-all-start) | async-done | bytes 524320 | tf_op jit(solution)/shard_map/all_to_all | solution.py:30
  35.9 0.8 copy-done.1
  36.6 3.8 %all-to-all-start.1 = ((bf16[32,8,4096]{2,1,0:T(8,128)(2,1)}), bf16[32,8,4096]{2,1,0:T(8,128)(2,1)S(1)}, u32[]{:S(2)}, u32[]{:S(2)}) async-start(bf16[32,8,4096]{2,1,0:T(8,128)(2,1)} %fusion.9), calls=%async_computation.1 | async-start | bytes 4194304 | tf_op jit(solution)/shard_map/all_to_all | solution.py:29
  40.4 0.0 all-gather.3.cloned.1.call-start
  40.5 0.7 all-gather.3.cloned.1.call-update
  41.2 0.0 reduce-scatter.2.cloned.1.call-start
  41.9 0.6 reduce_sum.134
  42.6 0.1 fusion.37
  42.7 0.1 convert_reduce_fusion
  42.8 0.1 fusion.40
  42.9 2.9 gather_fusion.1
  45.8 22.8 %all-to-all-done.1 = bf16[32,8,4096]{2,1,0:T(8,128)(2,1)S(1)} async-done(((bf16[32,8,4096]{2,1,0:T(8,128)(2,1)}), bf16[32,8,4096]{2,1,0:T(8,128)(2,1)S(1)}, u32[]{:S(2)}, u32[]{:S(2)}) %all-to-all-start.1) | async-done | bytes 2097184 | tf_op jit(solution)/shard_map/all_to_all | solution.py:29
  68.6 2.2 gather_fusion.3
  70.8 3.2 fusion.46
  73.9 0.1 fusion.47
  74.0 0.2 copy.36
  74.2 0.2 copy.37
  74.4 0.2 copy.38
  74.5 0.3 convolution_multiply_fusion.1
  74.8 0.3 fusion.48
  75.2 0.2 copy.41
  75.4 0.2 fusion.14
  75.6 0.1 copy-done.11
  75.6 3.9 %all-gather.5.cloned.1.call-done = bf16[512,1024]{1,0:T(8,128)(2,1)} async-done(((bf16[16,1024]{1,0:T(8,128)(2,1)}), bf16[512,1024]{1,0:T(8,128)(2,1)}) %all-gather.5.cloned.1.call-update) | async-done | bytes 1048592 | tf_op jit(solution)/shard_map/all_gather | solution.py:68
  79.5 1.5 fusion
  81.0 60.2 %all-gather.3.cloned.1.call-done = bf16[1024,1024]{1,0:T(8,128)(2,1)} async-done(((bf16[32,1024]{1,0:T(8,128)(2,1)}), bf16[1024,1024]{1,0:T(8,128)(2,1)}) %all-gather.3.cloned.1.call-update) | async-done | bytes 2097168 | tf_op jit(solution)/shard_map/all_gather | solution.py:63
  141.2 2.4 multiply_reduce_fusion.2
  143.6 0.8 copy-done.7
  144.4 2.5 select_reduce_fusion
  146.9 0.6 multiply_reduce_fusion.3
  147.5 103.9 %all-reduce = (f32[]{:T(128)}, f32[]{:T(128)}) all-reduce(f32[]{:T(128)} %get-tuple-element.9, f32[]{:T(128)} %reduce_sum.134), channel_id=1, replica_groups=mesh['grp'=16,'dev'=32] {'grp','dev'}, use_global_device_ids=true, to_apply=%region_8.9 | all-reduce | flops 2 | bytes 16 | tf_op jit(solution)/shard_map/psum | solution.py:129
  251.5 0.6 broadcast_divide_fusion
  252.1 2.8 convolution_convert_fusion
  254.9 2.2 multiply_reduce_fusion.1
  257.1 0.1 copy-done.6
  257.2 2.0 fusion.42
  259.3 1.0 fusion.19
  260.3 0.0 copy-done.15
  260.4 0.3 fusion.12
  260.7 0.0 reduce-scatter.2.cloned.1.call-update
  260.7 0.3 copy-done.16
  261.0 0.3 copy-done.9
  261.4 0.2 fusion.50
  262.9 0.2 copy.53
  263.1 0.3 fusion.49
  263.4 0.2 copy.52
  263.6 2.4 fusion.26
  266.0 2.0 copy.51
  268.1 3.0 fusion.8
  271.1 83.6 %reduce-scatter.2.cloned.1.call-done = bf16[16,1024]{1,0:T(8,128)(2,1)} async-done(((bf16[512,1024]{1,0:T(8,128)(2,1)}), bf16[16,1024]{1,0:T(8,128)(2,1)}) %reduce-scatter.2.cloned.1.call-update) | async-done | bytes 32784 | tf_op jit(solution)/shard_map/reduce_scatter | solution.py:94
  354.7 0.9 fusion.38
  355.6 1.5 fusion.39
  (48 shorter events, 0.1 us)
Async XLA Ops:
  7.2 17.0 %copy-start = (bf16[128,4096]{1,0:T(8,128)(2,1)S(1)}, bf16[128,4096]{1,0:T(8,128)(2,1)}, u32[]{:S(2)}) copy-start(bf16[128,4096]{1,0:T(8,128)(2,1)} %param.11) | copy-start | bytes 3145732
  7.2 72.3 %all-gather.5.cloned.1.call-start = ((), (), s32[]{:S(2)}) async-start(), calls=%async_computation.4 | async-start | bytes 1081344 | tf_op jit(solution)/shard_map/all_gather | solution.py:68
  13.7 22.2 %all-to-all-start = ((bf16[32,8,1024]{2,1,0:T(8,128)(2,1)}), bf16[32,8,1024]{2,1,0:T(8,128)(2,1)S(1)}, u32[]{:S(2)}, u32[]{:S(2)}) async-start(bf16[32,8,1024]{2,1,0:T(8,128)(2,1)} %fusion.15), calls=%async_computation | async-start | bytes 1048576 | tf_op jit(solution)/shard_map/all_to_all | solution.py:30
  30.6 11.3 %copy-start.20 = (f32[1,128]{1,0:T(1,128)S(1)}, f32[1,128]{1,0:T(1,128)}, u32[]{:S(2)}) copy-start(f32[1,128]{1,0:T(1,128)} %param.17) | copy-start | bytes 1540
  30.6 12.0 %copy-start.21 = (s32[1,128]{1,0:T(1,128)S(1)}, s32[1,128]{1,0:T(1,128)}, u32[]{:S(2)}) copy-start(s32[1,128]{1,0:T(1,128)} %param.14) | copy-start | bytes 1540
  30.6 12.0 %copy-start.13 = (bf16[16,1024]{1,0:T(8,128)(2,1)S(1)}, bf16[16,1024]{1,0:T(8,128)(2,1)}, u32[]{:S(2)}) copy-start(bf16[16,1024]{1,0:T(8,128)(2,1)} %param.19) | copy-start | bytes 98308
  30.6 12.1 %copy-start.18 = (s32[1,256]{1,0:T(1,128)S(1)}, s32[1,256]{1,0:T(1,128)}, u32[]{:S(2)}) copy-start(s32[1,256]{1,0:T(1,128)} %param.18) | copy-start | bytes 3076
  30.6 12.3 %copy-start.17 = (s32[1,128]{1,0:T(1,128)S(1)}, s32[1,128]{1,0:T(1,128)}, u32[]{:S(2)}) copy-start(s32[1,128]{1,0:T(1,128)} %param.15) | copy-start | bytes 1540
  35.8 0.8 copy-start.1
  36.6 32.0 %all-to-all-start.1 = ((bf16[32,8,4096]{2,1,0:T(8,128)(2,1)}), bf16[32,8,4096]{2,1,0:T(8,128)(2,1)S(1)}, u32[]{:S(2)}, u32[]{:S(2)}) async-start(bf16[32,8,4096]{2,1,0:T(8,128)(2,1)} %fusion.9), calls=%async_computation.1 | async-start | bytes 4194304 | tf_op jit(solution)/shard_map/all_to_all | solution.py:29
  40.4 100.8 %all-gather.3.cloned.1.call-start = ((), (), s32[]{:S(2)}) async-start(), calls=%async_computation.3 | async-start | bytes 2162688 | tf_op jit(solution)/shard_map/all_gather | solution.py:63
  41.2 313.5 %reduce-scatter.2.cloned.1.call-start = ((), (), s32[]{:S(2)}) async-start(), calls=%async_computation.5 | async-start | bytes 1081344 | tf_op jit(solution)/shard_map/reduce_scatter | solution.py:94
  74.2 1.0 copy-start.14
  74.3 0.8 copy-start.8
  74.8 0.8 copy-start.11
  74.8 66.4 %copy-start.10 = (bf16[128,1024]{1,0:T(8,128)(2,1)S(1)}, bf16[128,1024]{1,0:T(8,128)(2,1)}, u32[]{:S(2)}) copy-start(bf16[128,1024]{1,0:T(8,128)(2,1)} %gather_fusion.1) | copy-start | bytes 786436
  75.4 68.2 %copy-start.4 = (f32[128,1024]{1,0:T(8,128)}, f32[128,1024]{1,0:T(8,128)S(1)}, u32[]{:S(2)}) copy-start(f32[128,1024]{1,0:T(8,128)S(1)} %copy.41) | copy-start | bytes 1572868
  81.0 63.4 %copy-start.19 = (s32[1,128]{1,0:T(1,128)S(1)}, s32[1,128]{1,0:T(1,128)}, u32[]{:S(2)}) copy-start(s32[1,128]{1,0:T(1,128)} %param.16) | copy-start | bytes 1540
  143.6 0.8 copy-start.7
  252.1 5.0 %copy-start.3 = (bf16[1024,1024]{1,0:T(8,128)(2,1)S(1)}, bf16[1024,1024]{1,0:T(8,128)(2,1)}, u32[]{:S(2)}) copy-start(bf16[1024,1024]{1,0:T(8,128)(2,1)} %all-gather.3.cloned.1.call-done) | copy-start | bytes 6291460
  254.9 2.2 copy-start.5
  254.9 2.3 copy-start.6
  259.3 1.1 copy-start.12
  259.3 1.1 copy-start.15
  260.3 0.7 copy-start.16
  260.4 1.0 copy-start.9
  263.6 4.4 %copy-start.2 = (bf16[128,4096]{1,0:T(8,128)(2,1)S(1)}, bf16[128,4096]{1,0:T(8,128)(2,1)}, u32[]{:S(2)}) copy-start(bf16[128,4096]{1,0:T(8,128)(2,1)} %gather_fusion.3) | copy-start | bytes 3145732
Sparse Core Ops, SparseCore 0:
  11.1 68.2 all-gather.4
  82.6 58.5 all-gather.2
  260.9 93.7 reduce-scatter.1
where the time goes:
time: 366 us; the launch traced here: 365 us
  waiting for transfers between devices  177 us (48%)
  blocking collectives  104 us (28%)
  other arithmetic  19.8 us (5%)
  between operations  17.2 us (5%)
  local copies, waits for them, and re-layouts  16.6 us (5%)
  matrix products  15.7 us (4%)
  starting transfers between devices  14.3 us (4%)
    psum x1, blocking collectives, shards(): loss_sum = lax.psum(numerator, ('grp', 'dev'))  104 us
    reduce_scatter x1, waiting for transfers between devices, shards(): lax.psum_scatter(d_item.astype(jnp.bfloat16), 'dev', scatter_dimension=0,...  83.6 us
    all_gather x1, waiting for transfers between devices, shards(): weight_full = lax.all_gather(out_weight, 'dev', axis=0, tiled=True)  60.2 us
    all_to_all x1, waiting for transfers between devices, shards(): lax.all_to_all(send_proj, 'dev', split_axis=0, concat_axis=0, tiled=True)  22.8 us
    all_to_all x1, starting transfers between devices, shards(): lax.all_to_all(send_resid, 'dev', split_axis=0, concat_axis=0, tiled=True)  10.4 us
  transfers between devices with their start and end apart: 5, of which 5 were waited for; matrix products, arithmetic and copies ran while one was open for 9% of the time, Pallas kernels for 0%

commit v1 on v0

v1 whole, which is shorter than its diff:
```python
import jax
import jax.numpy as jnp
from jax import lax
from jax.experimental import pallas as pl
from jax.experimental.pallas import tpu as pltpu
from jax.sharding import Mesh, PartitionSpec as P

HEADS = 8
SHARP = 20.0
BF = jnp.bfloat16
F32 = jnp.float32
MEMBERS = ("x", "y", "c")
EVERY = ("z", "x", "y", "c")
PLANES = 4
SHIFTS = (0, 1, -1, 2)
PARAMS = dict(vmem_limit_bytes=32 * 1024 * 1024)


def dot_nn(a, b):
    return lax.dot_general(a, b, (((1,), (0,)), ((), ())), preferred_element_type=F32)


def dot_nt(a, b):
    return lax.dot_general(a, b, (((1,), (1,)), ((), ())), preferred_element_type=F32)


def dot_tn(a, b):
    return lax.dot_general(a, b, (((0,), (0,)), ((), ())), preferred_element_type=F32)


def sigmoid(values):
    return 1.0 / (1.0 + jnp.exp(-values))


def as_column(row):
    n = row.shape[1]
    return jnp.broadcast_to(row, (n, n)).T[:, :1]


def vmem(count):
    return [pl.BlockSpec(memory_space=pltpu.VMEM)] * count


def estimate(flops, nbytes, trans=0):
    return pl.CostEstimate(flops=flops, bytes_accessed=nbytes, transcendentals=trans)


def hbm(count):
    return [pl.BlockSpec(memory_space=pltpu.HBM)] * count


def in_hbm(*arrays):
    return [pltpu.with_memory_space_constraint(a, pltpu.HBM) for a in arrays]


def send_kernel(slots_in, proj_in, resid_in, out_ref, slots_ref, rows_ref, send_ref, in_sems, out_sems):
    rows, width = resid_in.shape
    slots = slots_ref.shape[1]
    parts = [slice(n * width, (n + 1) * width) for n in range(5)]
    first = pltpu.make_async_copy(slots_in, slots_ref, in_sems.at[5])
    first.start()
    into = []
    for n, part in enumerate(parts):
        source = resid_in if n == 4 else proj_in.at[:, part]
        into.append(pltpu.make_async_copy(source, rows_ref.at[:, part], in_sems.at[n]))
        into[-1].start()
    first.wait()
    ids = lax.broadcasted_iota(jnp.int32, (rows, slots), 0)
    pick = (ids == slots_ref[...]).astype(F32).T.astype(BF)
    out = []
    for n, part in enumerate(parts):
        into[n].wait()
        send_ref[:, part] = dot_nn(pick, rows_ref[:, part]).astype(BF)
        out.append(pltpu.make_async_copy(send_ref.at[:, part], out_ref.at[:, part], out_sems.at[n]))
        out[-1].start()
    for copy in out:
        copy.wait()


def send_blocks(slots, proj, resid):
    rows, width = resid.shape
    count = slots.shape[1]
    return pl.pallas_call(
        send_kernel,
        in_specs=hbm(3),
        out_specs=hbm(1)[0],
        out_shape=pltpu.HBM((count, 5 * width), BF),
        scratch_shapes=[
            pltpu.VMEM((1, count), jnp.int32),
            pltpu.VMEM((rows, 5 * width), BF),
            pltpu.VMEM((count, 5 * width), BF),
            pltpu.SemaphoreType.DMA((6,)),
            pltpu.SemaphoreType.DMA((5,)),
        ],
        compiler_params=pltpu.CompilerParams(**PARAMS),
        cost_estimate=estimate(2 * count * rows * 5 * width, 2 * 5 * width * (rows + count)),
        name="send_blocks",
    )(*in_hbm(slots, proj, resid))


def shared_kernel(table_in, weight_in, out_ref, table_ref, weight_ref, send_ref, sems):
    width = table_in.shape[1]
    size = weight_ref.shape[1]
    half = width // 2
    first = lax.rem(lax.axis_index("z"), width // size) * size
    into = [
        pltpu.make_async_copy(
            weight_in.at[:, pl.ds(pl.multiple_of(first, size), size)], weight_ref, sems.at[0]
        ),
        pltpu.make_async_copy(table_in, table_ref, sems.at[1]),
    ]
    for copy in into:
        copy.start()
    for copy in into:
        copy.wait()
    weight = weight_ref[...]
    table = table_ref[...].astype(F32)
    left, right = table[:, :half], table[:, half:]
    narrow = jnp.concatenate([left[:8], right[:8], left[8:], right[8:]], 0).astype(BF)
    for tile in range(send_ref.shape[0] // 32):
        send_ref[tile * 32 : (tile + 1) * 32, :size] = weight
        send_ref[tile * 32 : (tile + 1) * 32, size:] = narrow
    back = pltpu.make_async_copy(send_ref, out_ref, sems.at[2])
    back.start()
    back.wait()


def shared_blocks(table, weight, members):
    width = table.shape[1]
    size = width // PLANES
    shape = (members * 16, size + width // 2)
    return pl.pallas_call(
        shared_kernel,
        in_specs=hbm(2),
        out_specs=hbm(1)[0],
        out_shape=pltpu.HBM(shape, BF),
        scratch_shapes=[
            pltpu.VMEM(table.shape, BF),
            pltpu.VMEM((weight.shape[0], size), BF),
            pltpu.VMEM(shape, BF),
            pltpu.SemaphoreType.DMA((3,)),
        ],
        compiler_params=pltpu.CompilerParams(**PARAMS),
        cost_estimate=estimate(2 * shape[0] * shape[1], 2 * shape[0] * shape[1]),
        name="shared_blocks",
    )(*in_hbm(table, weight))


def weight_copies(near_in, far_in, weight_ref, sems):
    width = weight_ref.shape[3]
    size = width // PLANES
    z, core = lax.axis_index("z"), lax.axis_index("c")
    copies = []
    for source, side in ((near_in, core), (far_in, 1 - core)):
        for n, shift in enumerate(SHIFTS):
            first = pl.multiple_of(lax.rem(z + shift + PLANES, PLANES) * size, size)
            copies.append(
                pltpu.make_async_copy(
                    source.at[:, :, n * size : (n + 1) * size],
                    weight_ref.at[:, side, :, pl.ds(first, size)],
                    sems.at[len(copies)],
                )
            )
    return copies


def causal_mask(segment_row):
    n = segment_row.shape[1]
    spread = jnp.broadcast_to(segment_row.astype(F32), (n, n))
    rows = lax.broadcasted_iota(jnp.int32, (n, n), 0)
    cols = lax.broadcasted_iota(jnp.int32, (n, n), 1)
    return (spread == spread.T) & (cols <= rows)


def in_pieces(value):
    high = value.astype(BF).astype(F32)
    middle = (value - high).astype(BF).astype(F32)
    return high, middle, value - high - middle


def forward_kernel(
    order_ref, segments_ref, got_ref, near_in, far_in, negatives_ref, targets_ref, ratios_ref,
    topk_ref,
    grad_ref, invd_ref, inv_ref, ditem_out, user_out, item_out, pre_out, normed_out,
    pre_ref, normed_ref, resid_ref, ditem_ref, user_ref, item_ref, weight_ref, near_ref, far_ref,
    in_sems, out_sems,
):
    slots = got_ref.shape[0]
    rows, width = normed_ref.shape
    items = item_ref.shape[0]
    head = width // HEADS
    half = width // 2
    into = weight_copies(near_in, far_in, weight_ref, in_sems)
    into += [
        pltpu.make_async_copy(near_in.at[:, :, width:], near_ref, in_sems.at[2 * PLANES]),
        pltpu.make_async_copy(far_in.at[:, :, width:], far_ref, in_sems.at[2 * PLANES + 1]),
    ]
    for copy in into:
        copy.start()
    ids = lax.broadcasted_iota(jnp.int32, (slots, rows), 0)
    pick = (ids == order_ref[...]).astype(F32).T.astype(BF)
    for part in range(4):
        columns = slice(part * width, (part + 1) * width)
        pre_ref[:, columns] = dot_nn(pick, got_ref[:, columns]).astype(BF)
    resid_ref[...] = dot_nn(pick, got_ref[:, 4 * width :])
    save_pre = pltpu.make_async_copy(pre_ref, pre_out, out_sems.at[6])
    save_pre.start()
    mask = causal_mask(segments_ref[...])
    scaling = head ** (-0.5)

    def activated(part, h):
        start = part * width + h * head
        values = pre_ref[:, start : start + head].astype(F32)
        return values * sigmoid(values)

    for h in range(HEADS):
        value_h = activated(1, h).astype(BF)
        query_h = activated(2, h).astype(BF)
        key_h = activated(3, h).astype(BF)
        scores = dot_nt(query_h, key_h) * scaling
        att = jnp.where(mask, scores * sigmoid(scores), 0.0) * (2.0 / rows)
        normed_ref[:, h * head : (h + 1) * head] = dot_nn(att.astype(BF), value_h)
    mixed = normed_ref[...]
    centered = mixed - jnp.mean(mixed, 1, keepdims=True)
    inv_dev = lax.rsqrt(jnp.mean(centered * centered, 1, keepdims=True) + 1e-05)
    normed = centered * inv_dev
    normed_ref[...] = normed
    save_normed = pltpu.make_async_copy(normed_ref, normed_out, out_sems.at[7])
    save_normed.start()
    invd_ref[...] = inv_dev
    gate = pre_ref[:, :width].astype(F32)
    gated = (normed * (gate * sigmoid(gate))).astype(BF)
    for copy in into:
        copy.wait()
    weight = weight_ref[...].reshape(width, width)
    output = resid_ref[...] + dot_nn(gated, weight)
    inverse = lax.rsqrt(jnp.sum(output * output, 1, keepdims=True) + 1e-06)
    user = output * inverse
    user_ref[...] = user
    save_user = pltpu.make_async_copy(user_ref, user_out, out_sems.at[0])
    save_user.start()
    inv_ref[...] = inverse
    user_bf = user.astype(BF)
    drawn = negatives_ref.shape[1]
    hits = (lax.broadcasted_iota(jnp.int32, (items, drawn), 0) == negatives_ref[...]).astype(F32)
    counts = dot_nt(jnp.ones((8, drawn), BF), hits.astype(BF))[:1]
    ids = lax.broadcasted_iota(jnp.int32, (rows, items), 1)
    target = as_column(targets_ref[...].astype(F32)).astype(jnp.int32)
    onehot = jnp.where(ids == target, 1.0, 0.0)
    first = lax.axis_index("c") == 0
    near = near_ref[...].astype(F32)
    far = far_ref[...].astype(F32)
    near = jnp.concatenate([near[:, :8], near[:, 8:]], 2)
    far = jnp.concatenate([far[:, :8], far[:, 8:]], 2)
    low = jnp.where(first, near, far)
    high = jnp.where(first, far, near)
    values = jnp.concatenate([low, high], 1).reshape(items, width)
    item_inv = lax.rsqrt(jnp.sum(values * values, 1, keepdims=True) + 1e-06)
    item_ref[...] = (values * item_inv).astype(BF)
    save_item = pltpu.make_async_copy(item_ref, item_out, out_sems.at[1])
    save_item.start()
    logits = SHARP * dot_nt(user_bf, item_ref[...])
    mass = (counts + onehot) * jnp.exp(logits)
    totals = jnp.sum(mass, 1, keepdims=True)
    positive = jnp.sum(onehot * logits, 1, keepdims=True)
    rest = 1.0 - jnp.exp(positive) / totals
    row_loss = jnp.log(totals) - positive
    size = topk_ref[0]
    power = jnp.ones_like(rest)
    square = rest
    for bit in range(4):
        power = jnp.where((((size - 1) >> bit) & 1) == 1, power * square, power)
        square = square * square
    ratio = as_column(ratios_ref[...])
    row_weight = ratio * (size.astype(F32) * power)
    grad = (SHARP * row_weight) * (mass / totals - onehot)
    grad_bf = grad.astype(BF)
    grad_ref[...] = grad_bf
    numerator = jnp.sum(row_weight * row_loss, 0, keepdims=True)
    lanes = lax.broadcasted_iota(jnp.int32, (items, 128), 1)
    extra = jnp.zeros((items, 128), F32)
    pieces = in_pieces(numerator) + in_pieces(jnp.sum(ratio, 0, keepdims=True))
    for lane, piece in enumerate(pieces):
        extra = jnp.where(lanes == lane, piece, extra)
    ditem_ref[:, width:] = extra.astype(BF)
    out = []
    steps = 4
    for step in range(steps):
        at = slice(step * items // steps, (step + 1) * items // steps)
        ditem_ref[at, :width] = dot_tn(grad_bf[:, at], user_bf).astype(BF)
        out.append(
            pltpu.make_async_copy(ditem_ref.at[at, :], ditem_out.at[at, :], out_sems.at[2 + step])
        )
        out[-1].start()
    for copy in [save_user, save_item, save_pre, save_normed] + out:
        copy.wait()


def forward_pass(order, segments, got, near, far, negatives, targets, ratios, topk):
    rows = order.shape[1]
    width = got.shape[1] // 5
    members, block = near.shape[:2]
    items = members * block
    return pl.pallas_call(
        forward_kernel,
        in_specs=vmem(3) + hbm(2) + vmem(3) + [pl.BlockSpec(memory_space=pltpu.SMEM)],
        out_specs=vmem(3) + hbm(5),
        out_shape=[
            jax.ShapeDtypeStruct((rows, items), BF),
            jax.ShapeDtypeStruct((rows, 1), F32),
            jax.ShapeDtypeStruct((rows, 1), F32),
            pltpu.HBM((items, width + 128), BF),
            pltpu.HBM((rows, width), F32),
            pltpu.HBM((items, width), BF),
            pltpu.HBM((rows, 4 * width), BF),
            pltpu.HBM((rows, width), F32),
        ],
        scratch_shapes=[
            pltpu.VMEM((rows, 4 * width), BF),
            pltpu.VMEM((rows, width), F32),
            pltpu.VMEM((rows, width), F32),
            pltpu.VMEM((items, width + 128), BF),
            pltpu.VMEM((rows, width), F32),
            pltpu.VMEM((items, width), BF),
            pltpu.VMEM((members, 2, block, width), BF),
            pltpu.VMEM((members, block, width // 2), BF),
            pltpu.VMEM((members, block, width // 2), BF),
            pltpu.SemaphoreType.DMA((2 * PLANES + 2,)),
            pltpu.SemaphoreType.DMA((8,)),
        ],
        compiler_params=pltpu.CompilerParams(**PARAMS),
        cost_estimate=estimate(2 * rows * width * 3328, 12 * 1024 * 1024),
        name="forward_pass",
    )(order, segments, got, *in_hbm(near, far), negatives, targets, ratios, topk)


def back_kernel(
    pre_ref, normed_ref, invd_ref, segments_ref, grad_ref, user_ref, invo_ref, item_ref, near_in, far_in,
    out_ref, weight_ref, sems,
):
    rows, width = normed_ref.shape
    head = width // HEADS
    into = weight_copies(near_in, far_in, weight_ref, sems)
    for copy in into:
        copy.start()
    user = user_ref[...]
    d_user = dot_nn(grad_ref[...], item_ref[...])
    d_output = invo_ref[...] * (d_user - user * jnp.sum(user * d_user, 1, keepdims=True))
    for copy in into:
        copy.wait()
    d_gated = dot_nt(d_output.astype(BF), weight_ref[...].reshape(width, width))
    normed = normed_ref[...]
    gate = pre_ref[:, :width].astype(F32)
    gate_s = sigmoid(gate)
    d_normed = d_gated * (gate * gate_s)
    d_gate = d_gated * normed
    out_ref[:, :width] = d_gate * (gate_s * (1.0 + gate * (1.0 - gate_s)))
    d_mixed = invd_ref[...] * (
        d_normed
        - jnp.mean(d_normed, 1, keepdims=True)
        - normed * jnp.mean(d_normed * normed, 1, keepdims=True)
    )
    dmix_bf = d_mixed.astype(BF)
    mask = causal_mask(segments_ref[...])
    scaling = head ** (-0.5)

    def opened(part, h):
        start = part * width + h * head
        values = pre_ref[:, start : start + head].astype(F32)
        logistic = sigmoid(values)
        slope = logistic * (1.0 + values * (1.0 - logistic))
        return (values * logistic).astype(BF), slope

    for h in range(HEADS):
        value_h, value_slope = opened(1, h)
        query_h, query_slope = opened(2, h)
        key_h, key_slope = opened(3, h)
        scores = dot_nt(query_h, key_h) * scaling
        logistic = sigmoid(scores)
        att = jnp.where(mask, scores * logistic, 0.0) * (2.0 / rows)
        dmix_h = dmix_bf[:, h * head : (h + 1) * head]
        d_att = dot_nt(dmix_h, value_h)
        d_value = dot_tn(att.astype(BF), dmix_h)
        slope = logistic * (1.0 + scores * (1.0 - logistic))
        d_scores = jnp.where(mask, d_att * slope, 0.0) * (scaling * 2.0 / rows)
        d_scores = d_scores.astype(BF)
        d_query = dot_nn(d_scores, key_h)
        d_key = dot_tn(d_scores, query_h)
        for part, grad, rate in (
            (1, d_value, value_slope), (2, d_query, query_slope), (3, d_key, key_slope)
        ):
            start = part * width + h * head
            out_ref[:, start : start + head] = grad * rate


def back_pass(pre, normed, inv_dev, segments, grad, user, inv_out, item, near, far):
    rows, width = normed.shape
    members, block = near.shape[:2]
    return pl.pallas_call(
        back_kernel,
        in_specs=vmem(8) + hbm(2),
        out_specs=pl.BlockSpec(memory_space=pltpu.VMEM),
        out_shape=jax.ShapeDtypeStruct((rows, 4 * width), F32),
        scratch_shapes=[
            pltpu.VMEM((members, 2, block, width), BF),
            pltpu.SemaphoreType.DMA((2 * PLANES,)),
        ],
        compiler_params=pltpu.CompilerParams(**PARAMS),
        cost_estimate=estimate(2 * rows * width * 2304, 8 * 1024 * 1024),
        name="back_pass",
    )(pre, normed, inv_dev, segments, grad, user, inv_out, item, *in_hbm(near, far))


def table_kernel(got_ref, table_ref, out_ref, sums_ref):
    width = table_ref.shape[1]
    summed = jnp.sum(got_ref[:, :, :width].astype(F32), 0)
    own = table_ref[...].astype(F32)
    inverse = lax.rsqrt(jnp.sum(own * own, 1, keepdims=True) + 1e-06)
    item = own * inverse
    inner = jnp.sum(item * summed, 1, keepdims=True)
    out_ref[...] = inverse * (summed - item * inner)
    extra = jnp.sum(got_ref[:, :, width:].astype(F32), 0)[:8]
    sums_ref[...] = jnp.broadcast_to(extra[None], sums_ref.shape)


def table_pass(got, table, groups):
    return pl.pallas_call(
        table_kernel,
        in_specs=vmem(2),
        out_specs=vmem(2),
        out_shape=[
            jax.ShapeDtypeStruct(table.shape, F32),
            jax.ShapeDtypeStruct((groups, 8, 128), F32),
        ],
        compiler_params=pltpu.CompilerParams(**PARAMS),
        cost_estimate=estimate(got.size * 2, got.size * 2),
        name="table_pass",
    )(got, table)


def finish_kernel(sums_ref, act_ref, table_ref, loss_ref, proj_out, out_ref, proj_ref, sems):
    row = jnp.sum(sums_ref[...], 0)[:1]
    lanes = lax.broadcasted_iota(jnp.int32, row.shape, 1)
    numerator = jnp.sum(jnp.where(lanes < 3, row, 0.0), 1, keepdims=True)
    total = jnp.sum(jnp.where(lanes < 3, 0.0, row), 1, keepdims=True)
    share = 1.0 / total
    steps = 4
    size = act_ref.shape[0] // steps
    out = []
    for step in range(steps):
        at = slice(step * size, (step + 1) * size)
        proj_ref[at, :] = (act_ref[at, :] * share).astype(BF)
        out.append(
            pltpu.make_async_copy(proj_ref.at[at, :], proj_out.at[at, :], sems.at[step])
        )
        out[-1].start()
    loss_ref[...] = jnp.broadcast_to(numerator * share, loss_ref.shape)
    out_ref[...] = table_ref[...] * share
    for copy in out:
        copy.wait()


def finish(sums, d_act, d_table):
    rows, columns = d_act.shape
    return pl.pallas_call(
        finish_kernel,
        in_specs=vmem(3),
        out_specs=vmem(1) + hbm(1) + vmem(1),
        out_shape=[
            jax.ShapeDtypeStruct((1, 128), F32),
            jax.ShapeDtypeStruct((rows, columns), BF),
            jax.ShapeDtypeStruct(d_table.shape, F32),
        ],
        scratch_shapes=[pltpu.VMEM((rows, columns), BF), pltpu.SemaphoreType.DMA((4,))],
        compiler_params=pltpu.CompilerParams(**PARAMS),
        cost_estimate=estimate(rows * columns, rows * columns * 6),
        name="finish",
    )(sums, d_act, d_table)


def shards(
    proj, resid, send_rows, pack_rows, segments, targets, ratios, negatives, table, out_weight, topk,
    *, groups, members,
):
    width = resid.shape[1]
    mine = table.shape[0]
    with jax.named_scope("shared"):
        share = shared_blocks(table, out_weight, members)
        share = lax.all_to_all(
            share.reshape(members, mine, share.shape[1]), MEMBERS, 0, 0, tiled=True
        )
    with jax.named_scope("route"):
        send = send_blocks(send_rows, proj, resid)
        got = lax.all_to_all(
            send.reshape(members, -1, 5 * width), MEMBERS, 0, 0, tiled=True
        ).reshape(send.shape)
    with jax.named_scope("planes"):
        size = width // PLANES
        mine_part = share[:, :, :size]
        parts = [mine_part]
        for shift in SHIFTS[1:]:
            pairs = [(i, (i - shift) % groups) for i in range(groups)]
            parts.append(lax.ppermute(mine_part, "z", pairs))
        near = jnp.concatenate(parts + [share[:, :, size:]], 2)
        far = lax.ppermute(near, "c", [(0, 1), (1, 0)])
    grad, inv_dev, inv_out, d_item, user, item, pre, normed = forward_pass(
        pack_rows, segments, got, near, far, negatives, targets, ratios, topk
    )
    with jax.named_scope("items_back"):
        got_item = lax.all_to_all(
            d_item.reshape(members, mine, width + 128), MEMBERS, 0, 0, tiled=True
        )
    d_act = back_pass(pre, normed, inv_dev, segments, grad, user, inv_out, item, near, far)
    d_table, sums = table_pass(got_item, table, groups)
    with jax.named_scope("sums"):
        sums = lax.all_to_all(sums, "z", 0, 0, tiled=True)
    loss, d_proj, d_table = finish(sums, d_act, d_table)
    return (loss[0, :1], d_proj, d_table)


def solution(mesh):
    groups, members = mesh.devices.shape
    side = 4
    fine = Mesh(
        mesh.devices.reshape(groups, side, members // (2 * side), 2), ("z", "x", "y", "c")
    )

    def body(*args):
        return shards(*args, groups=groups, members=members)

    return jax.shard_map(
        body,
        mesh=fine,
        in_specs=(
            P(EVERY, None),
            P(EVERY, None),
            P(EVERY, None),
            P(EVERY, None),
            P(EVERY, None),
            P(EVERY, None),
            P(EVERY, None),
            P("z", None),
            P(EVERY, None),
            P(MEMBERS, None),
            P(),
        ),
        out_specs=(P(), P(EVERY, None), P(EVERY, None)),
        check_vma=False,
    )
```

time: 366 us -> 122 us (0.33)
  waiting for transfers between devices: 177 us -> 25.8 us
  blocking collectives: 104 us -> 26.3 us
  starting transfers between devices: 14.3 us -> 42.9 us
  other arithmetic: 19.8 us -> 0 us
  Pallas kernels: 0 us -> 17.6 us
  between operations: 17.2 us -> 1.48 us
  matrix products: 15.7 us -> 0 us
  local copies, waits for them, and re-layouts: 16.6 us -> 7.34 us
    psum x1 -> x0, blocking collectives: 104 us -> none  [shards(): loss_sum = lax.psum(numerator, ('grp', 'dev'))]
    reduce_scatter x1 -> x0, waiting for transfers between devices: 83.6 us -> none  [shards(): lax.psum_scatter(d_item.astype(jnp.bfloat16), 'dev', scatter_dimension=0,...]
    all_gather x2 -> x0, waiting for transfers between devices: 64.1 us -> none  [the longest x1 60.2 us: shards(): weight_full = lax.all_gather(out_weight, 'dev', axis=0, tiled=True)]
    all_to_all x0 -> x1, blocking collectives: none -> 26.3 us  [shards(): lax.all_to_all(d_item.reshape(members, mine, width + 128), MEMBERS, 0, 0,...]
    ppermute x0 -> x4, starting transfers between devices: none -> 18.1 us  [the longest x3 14.9 us: shards(): parts.append(lax.ppermute(mine_part, 'z', pairs))]
    pallas_call x0 -> x6, Pallas kernels: none -> 17.6 us  [the longest x1 5.43 us: forward_pass(): pl.pallas_call(forward_kernel, in_specs=vmem(3) + hbm(2) + vmem(3) + [pl....]
    dot_general x11 -> x0, matrix products: 15.7 us -> none  [the longest x1 2.84 us: shards(): jnp.einsum('tm,td->md', grad_bf, user_bf, preferred_element_type=jnp.floa...]
    gather x4 -> x0, local copies, waits for them, and re-layouts: 10.8 us -> none  [the longest x1 3.2 us: shards(): jnp.take(proj, clipped, axis=0)]
  transfers between devices with their start and end apart: 5 -> 7, of which waited for: 5 -> 5; matrix products, arithmetic and copies ran while one was open for 9% -> 3% of each run, Pallas kernels for 0% -> 6%
where the time goes in v1:
time: 122 us; the launch traced here: 121 us
  starting transfers between devices  42.9 us (35%)
  blocking collectives  26.3 us (22%)
  waiting for transfers between devices  25.8 us (21%)
  Pallas kernels  17.6 us (14%)
  local copies, waits for them, and re-layouts  7.34 us (6%)
  between operations  1.48 us (1%)
    all_to_all x1, blocking collectives, shards(): lax.all_to_all(d_item.reshape(members, mine, width + 128), MEMBERS, 0, 0,...  26.3 us
    ppermute x3, starting transfers between devices, shards(): parts.append(lax.ppermute(mine_part, 'z', pairs))  14.9 us
    all_to_all x1, waiting for transfers between devices, shards(): lax.all_to_all(share.reshape(members, mine, share.shape[1]), MEMBERS, 0,...  11 us
    all_to_all x1, starting transfers between devices, shards(): sums = lax.all_to_all(sums, 'z', 0, 0, tiled=True)  10.5 us
    all_to_all x1, starting transfers between devices, shards(): lax.all_to_all(share.reshape(members, mine, share.shape[1]), MEMBERS, 0,...  10.5 us
    ppermute x3, waiting for transfers between devices, shards(): parts.append(lax.ppermute(mine_part, 'z', pairs))  8.09 us
    unnamed x23, local copies, waits for them, and re-layouts  5.64 us
    pallas_call x1, Pallas kernels, forward_pass(): pl.pallas_call(forward_kernel, in_specs=vmem(3) + hbm(2) + vmem(3) + [pl....  5.43 us
  transfers between devices with their start and end apart: 7, of which 5 were waited for; matrix products, arithmetic and copies ran while one was open for 3% of the time, Pallas kernels for 6%

profile of v1, /device:TPU:1, one launch (start us, length us, event | category | flops | bytes accessed | tf_op | source)
XLA Modules:
  0.0 121.4 jit_solution(2663413395536301376)
XLA Ops:
  0.6 1.8 %shared_blocks.1 = bf16[512,768]{1,0:T(8,128)(2,1)} custom-call(bf16[16,1024]{1,0:T(8,128)(2,1)} %table_ref.1, bf16[32,1024]{1,0:T(8,128)(2,1)} %weight_in.1), custom_call_target="tpu_custom_call" | custom-call | flops 786432 | bytes 786432 | tf_op jit(solution)/shard_map/shared/shared_blocks/pallas_call | solution.py:132
  2.4 10.5 %all-to-all-start.1 = ((bf16[32,16,768]{2,1,0:T(8,128)(2,1)}), bf16[32,16,768]{2,1,0:T(8,128)(2,1)S(1)}, u32[]{:S(2)}, u32[]{:S(2)}) async-start(bf16[32,16,768]{2,1,0:T(8,128)(2,1)} %bitcast.8), calls=%async_computation.1 | async-start | bytes 1572864 | tf_op jit(solution)/shard_map/shared/all_to_all | solution.py:489
  12.9 3.3 %send_blocks.1 = bf16[256,5120]{1,0:T(8,128)(2,1)} custom-call(s32[1,256]{1,0:T(1,128)} %slots_in.1, bf16[128,4096]{1,0:T(8,128)(2,1)} %proj_in.1, bf16[128,1024]{1,0:T(8,128)(2,1)} %resid_in.1), custom_call_target="tpu_custom_call" | custom-call | flops 335544320 | bytes 3932160 | tf_op jit(solution)/shard_map/route/send_blocks/pallas_call | solution.py:83
  16.2 11.0 %all-to-all-done.1 = bf16[32,16,768]{2,1,0:T(8,128)(2,1)S(1)} async-done(((bf16[32,16,768]{2,1,0:T(8,128)(2,1)}), bf16[32,16,768]{2,1,0:T(8,128)(2,1)S(1)}, u32[]{:S(2)}, u32[]{:S(2)}) %all-to-all-start.1) | async-done | bytes 786464 | tf_op jit(solution)/shard_map/shared/all_to_all | solution.py:489
  27.2 3.8 %all-to-all-start = ((bf16[32,8,5120]{2,1,0:T(8,128)(2,1)}), bf16[32,8,5120]{2,1,0:T(8,128)(2,1)S(1)}, u32[]{:S(2)}, u32[]{:S(2)}) async-start(bf16[32,8,5120]{2,1,0:T(8,128)(2,1)} %bitcast.7), calls=%async_computation | async-start | bytes 5242880 | tf_op jit(solution)/shard_map/route/all_to_all | solution.py:494
  31.1 0.0 copy-start.5
  31.1 0.0 copy-start.6
  31.1 0.0 copy-start.7
  31.1 0.0 copy-start.8
  31.1 0.0 copy-start.9
  31.1 0.8 fusion
  31.9 9.1 %collective-permute-start = (bf16[32,16,256]{2,1,0:T(8,128)(2,1)S(1)}, bf16[32,16,256]{2,1,0:T(8,128)(2,1)S(1)}, u32[]{:S(2)}, u32[]{:S(2)}) collective-permute-start(bf16[32,16,256]{2,1,0:T(8,128)(2,1)S(1)} %get-tuple-element.29), channel_id=1, source_target_pairs={{0,480},{32,0},{64,32},{96,64},{128,96},{160,128},{192,160},{224,1... | collective-permute-start | bytes 786440 | tf_op jit(solution)/shard_map/planes/ppermute | solution.py:503
  41.1 1.9 %collective-permute-start.1 = (bf16[32,16,256]{2,1,0:T(8,128)(2,1)S(1)}, bf16[32,16,256]{2,1,0:T(8,128)(2,1)S(1)}, u32[]{:S(2)}, u32[]{:S(2)}) collective-permute-start(bf16[32,16,256]{2,1,0:T(8,128)(2,1)S(1)} %get-tuple-element.29), channel_id=1, source_target_pairs={{0,32},{32,64},{64,96},{96,128},{128,160},{160,192},{192,224},{224... | collective-permute-start | bytes 786440 | tf_op jit(solution)/shard_map/planes/ppermute | solution.py:503
  43.0 3.8 %collective-permute-start.2 = (bf16[32,16,256]{2,1,0:T(8,128)(2,1)S(1)}, bf16[32,16,256]{2,1,0:T(8,128)(2,1)S(1)}, u32[]{:S(2)}, u32[]{:S(2)}) collective-permute-start(bf16[32,16,256]{2,1,0:T(8,128)(2,1)S(1)} %get-tuple-element.29), channel_id=1, source_target_pairs={{0,448},{32,480},{64,0},{96,32},{128,64},{160,96},{192,128},{224,1... | collective-permute-start | bytes 786440 | tf_op jit(solution)/shard_map/planes/ppermute | solution.py:503
  46.8 0.0 collective-permute-done
  46.8 0.8 constant_dynamic-update-slice_fusion.2
  47.6 3.9 %collective-permute-done.1 = bf16[32,16,256]{2,1,0:T(8,128)(2,1)S(1)} collective-permute-done((bf16[32,16,256]{2,1,0:T(8,128)(2,1)S(1)}, bf16[32,16,256]{2,1,0:T(8,128)(2,1)S(1)}, u32[]{:S(2)}, u32[]{:S(2)}) %collective-permute-start.1) | collective-permute-done | bytes 262176 | tf_op jit(solution)/shard_map/planes/ppermute | solution.py:503
  51.5 0.7 constant_dynamic-update-slice_fusion.1
  52.3 4.1 %collective-permute-done.2 = bf16[32,16,256]{2,1,0:T(8,128)(2,1)S(1)} collective-permute-done((bf16[32,16,256]{2,1,0:T(8,128)(2,1)S(1)}, bf16[32,16,256]{2,1,0:T(8,128)(2,1)S(1)}, u32[]{:S(2)}, u32[]{:S(2)}) %collective-permute-start.2) | collective-permute-done | bytes 262176 | tf_op jit(solution)/shard_map/planes/ppermute | solution.py:503
  56.4 0.8 constant_dynamic-update-slice_fusion
  57.2 0.9 slice_dynamic-update-slice_fusion.near_in
  58.1 3.2 %collective-permute-start.3 = (bf16[32,16,1536]{2,1,0:T(8,128)(2,1)}, bf16[32,16,1536]{2,1,0:T(8,128)(2,1)}, u32[]{:S(2)}, u32[]{:S(2)}) collective-permute-start(bf16[32,16,1536]{2,1,0:T(8,128)(2,1)} %slice_dynamic-update-slice_fusion.near_in), channel_id=1, source_target_pairs={{0,1},{1,0},{2,3},{3,2},{4,5},{5,4},{6,7},{7,6},{8,9},{9,8},{10,11... | collective-permute-start | bytes 4718600 | tf_op jit(solution)/shard_map/planes/ppermute | solution.py:505
  62.0 2.9 %all-to-all-done = bf16[32,8,5120]{2,1,0:T(8,128)(2,1)S(1)} async-done(((bf16[32,8,5120]{2,1,0:T(8,128)(2,1)}), bf16[32,8,5120]{2,1,0:T(8,128)(2,1)S(1)}, u32[]{:S(2)}, u32[]{:S(2)}) %all-to-all-start) | async-done | bytes 2621472 | tf_op jit(solution)/shard_map/route/all_to_all | solution.py:494
  64.9 0.0 collective-permute-done.3.far_in
  64.9 0.0 copy-done.5
  64.9 0.0 copy-done.6
  64.9 0.0 copy-done.7
  64.9 0.0 copy-done.8
  64.9 0.0 copy-done.9
  64.9 5.4 %forward_pass.1 = (bf16[128,512]{1,0:T(8,128)(2,1)S(1)}, f32[128,1]{1,0:T(8,128)S(1)}, f32[128,1]{1,0:T(8,128)S(1)}, bf16[512,1152]{1,0:T(8,128)(2,1)}, f32[128,...) custom-call(s32[1,128]{1,0:T(1,128)S(1)} %copy-done.7, ...), custom_call_target="tpu_custom_call" | custom-call | flops 872415232 | bytes 12582912 | tf_op jit(solution)/shard_map/forward_pass/pallas_call | solution.py:304
  70.4 0.0 copy-start.4
  70.4 0.0 copy-start
  70.4 26.3 %all_to_all.20.got_ref = bf16[32,16,1152]{2,1,0:T(8,128)(2,1)S(1)} all-to-all(bf16[32,16,1152]{2,1,0:T(8,128)(2,1)} %bitcast.9), channel_id=1, replica_groups=mesh['z'=16,'x'=4,'y'=4,'c'=2] {'x','y','c'}, dimensions={0} | all-to-all | bytes 2359296 | tf_op jit(solution)/shard_map/items_back/all_to_all | solution.py:510
  96.6 0.0 copy-done.4
  96.7 0.8 table_pass.1
  97.5 10.5 %all-to-all-start.3 = ((f32[16,8,128]{2,1,0:T(8,128)}), f32[16,8,128]{2,1,0:T(8,128)S(1)}, u32[]{:S(2)}, u32[]{:S(2)}) async-start(f32[16,8,128]{2,1,0:T(8,128)} %get-tuple-element.17), calls=%async_computation.3 | async-start | bytes 131072 | tf_op jit(solution)/shard_map/sums/all_to_all | solution.py:516
  108.0 0.0 copy-done
  108.1 0.0 copy-start.1
  108.1 1.2 %copy-done.1 = bf16[128,4096]{1,0:T(8,128)(2,1)S(1)} copy-done((bf16[128,4096]{1,0:T(8,128)(2,1)S(1)}, bf16[128,4096]{1,0:T(8,128)(2,1)}, u32[]{:S(2)}) %copy-start.1) | copy-done | bytes 1048600
  109.3 0.0 copy-start.2
  109.3 1.0 copy-done.2
  110.3 0.0 copy-start.3
  110.3 1.0 copy-done.3
  111.4 4.5 %back_pass.1.act_ref = f32[128,4096]{1,0:T(8,128)S(1)} custom-call(bf16[128,4096]{1,0:T(8,128)(2,1)S(1)} %copy-done.1, f32[128,1024]{1,0:T(8,128)S(1)} %copy-done.3, f32[128,1]{1,0:T(8,128)S(1)} %get-tuple-element.20.invd_ref, s32[1,128]{1,0:T(1,128)S(1)} %copy-done.5, bf16[128,512]{1,0:T(8,128)(2,1)S(1)} %get-tuple-element.21.grad_ref, ...), custom_call_target="tpu_custom_call" | custom-call | flops 603979776 | bytes 8388608 | tf_op jit(solution)/shard_map/back_pass/pallas_call | solution.py:399
  115.8 3.8 %all-to-all-done.3.sums_ref = f32[16,8,128]{2,1,0:T(8,128)S(1)} async-done(((f32[16,8,128]{2,1,0:T(8,128)}), f32[16,8,128]{2,1,0:T(8,128)S(1)}, u32[]{:S(2)}, u32[]{:S(2)}) %all-to-all-start.3) | async-done | bytes 65568 | tf_op jit(solution)/shard_map/sums/all_to_all | solution.py:516
  119.6 1.8 %finish.1 = (f32[1,128]{1,0:T(1,128)}, bf16[128,4096]{1,0:T(8,128)(2,1)}, f32[16,1024]{1,0:T(8,128)}) custom-call(f32[16,8,128]{2,1,0:T(8,128)S(1)} %all-to-all-done.3.sums_ref, f32[128,4096]{1,0:T(8,128)S(1)} %back_pass.1.act_ref, f32[16,1024]{1,0:T(8,128)S(1)} %get-tuple-element.25.table_ref), custom_call_target="tpu_custom_call" | custom-call | flops 524288 | bytes 3145728 | tf_op jit(solution)/shard_map/finish/pallas_call | solution.py:465
Async XLA Ops:
  2.4 24.8 %all-to-all-start.1 = ((bf16[32,16,768]{2,1,0:T(8,128)(2,1)}), bf16[32,16,768]{2,1,0:T(8,128)(2,1)S(1)}, u32[]{:S(2)}, u32[]{:S(2)}) async-start(bf16[32,16,768]{2,1,0:T(8,128)(2,1)} %bitcast.8), calls=%async_computation.1 | async-start | bytes 1572864 | tf_op jit(solution)/shard_map/shared/all_to_all | solution.py:489
  27.2 37.7 %all-to-all-start = ((bf16[32,8,5120]{2,1,0:T(8,128)(2,1)}), bf16[32,8,5120]{2,1,0:T(8,128)(2,1)S(1)}, u32[]{:S(2)}, u32[]{:S(2)}) async-start(bf16[32,8,5120]{2,1,0:T(8,128)(2,1)} %bitcast.7), calls=%async_computation | async-start | bytes 5242880 | tf_op jit(solution)/shard_map/route/all_to_all | solution.py:494
  31.1 33.8 %copy-start.5 = (s32[1,128]{1,0:T(1,128)S(1)}, s32[1,128]{1,0:T(1,128)}, u32[]{:S(2)}) copy-start(s32[1,128]{1,0:T(1,128)} %segments_ref.3) | copy-start | bytes 1540
  31.1 33.8 %copy-start.6 = (s32[1,256]{1,0:T(1,128)S(1)}, s32[1,256]{1,0:T(1,128)}, u32[]{:S(2)}) copy-start(s32[1,256]{1,0:T(1,128)} %negatives_ref.1) | copy-start | bytes 3076
  31.1 33.8 %copy-start.7 = (s32[1,128]{1,0:T(1,128)S(1)}, s32[1,128]{1,0:T(1,128)}, u32[]{:S(2)}) copy-start(s32[1,128]{1,0:T(1,128)} %order_ref.1) | copy-start | bytes 1540
  31.1 33.8 %copy-start.8 = (s32[1,128]{1,0:T(1,128)S(1)}, s32[1,128]{1,0:T(1,128)}, u32[]{:S(2)}) copy-start(s32[1,128]{1,0:T(1,128)} %targets_ref.1) | copy-start | bytes 1540
  31.1 33.8 %copy-start.9 = (f32[1,128]{1,0:T(1,128)S(1)}, f32[1,128]{1,0:T(1,128)}, u32[]{:S(2)}) copy-start(f32[1,128]{1,0:T(1,128)} %ratios_ref.1) | copy-start | bytes 1540
  31.9 14.9 %collective-permute-start = (bf16[32,16,256]{2,1,0:T(8,128)(2,1)S(1)}, bf16[32,16,256]{2,1,0:T(8,128)(2,1)S(1)}, u32[]{:S(2)}, u32[]{:S(2)}) collective-permute-start(bf16[32,16,256]{2,1,0:T(8,128)(2,1)S(1)} %get-tuple-element.29), channel_id=1, source_target_pairs={{0,480},{32,0},{64,32},{96,64},{128,96},{160,128},{192,160},{224,1... | collective-permute-start | bytes 786440 | tf_op jit(solution)/shard_map/planes/ppermute | solution.py:503
  41.1 10.5 %collective-permute-start.1 = (bf16[32,16,256]{2,1,0:T(8,128)(2,1)S(1)}, bf16[32,16,256]{2,1,0:T(8,128)(2,1)S(1)}, u32[]{:S(2)}, u32[]{:S(2)}) collective-permute-start(bf16[32,16,256]{2,1,0:T(8,128)(2,1)S(1)} %get-tuple-element.29), channel_id=1, source_target_pairs={{0,32},{32,64},{64,96},{96,128},{128,160},{160,192},{192,224},{224... | collective-permute-start | bytes 786440 | tf_op jit(solution)/shard_map/planes/ppermute | solution.py:503
  43.0 13.4 %collective-permute-start.2 = (bf16[32,16,256]{2,1,0:T(8,128)(2,1)S(1)}, bf16[32,16,256]{2,1,0:T(8,128)(2,1)S(1)}, u32[]{:S(2)}, u32[]{:S(2)}) collective-permute-start(bf16[32,16,256]{2,1,0:T(8,128)(2,1)S(1)} %get-tuple-element.29), channel_id=1, source_target_pairs={{0,448},{32,480},{64,0},{96,32},{128,64},{160,96},{192,128},{224,1... | collective-permute-start | bytes 786440 | tf_op jit(solution)/shard_map/planes/ppermute | solution.py:503
  58.1 6.8 %collective-permute-start.3 = (bf16[32,16,1536]{2,1,0:T(8,128)(2,1)}, bf16[32,16,1536]{2,1,0:T(8,128)(2,1)}, u32[]{:S(2)}, u32[]{:S(2)}) collective-permute-start(bf16[32,16,1536]{2,1,0:T(8,128)(2,1)} %slice_dynamic-update-slice_fusion.near_in), channel_id=1, source_target_pairs={{0,1},{1,0},{2,3},{3,2},{4,5},{5,4},{6,7},{7,6},{8,9},{9,8},{10,11... | collective-permute-start | bytes 4718600 | tf_op jit(solution)/shard_map/planes/ppermute | solution.py:505
  70.4 26.3 %copy-start.4 = (bf16[16,1024]{1,0:T(8,128)(2,1)S(1)}, bf16[16,1024]{1,0:T(8,128)(2,1)}, u32[]{:S(2)}) copy-start(bf16[16,1024]{1,0:T(8,128)(2,1)} %table_ref.1) | copy-start | bytes 98308
  70.4 37.7 %copy-start = (bf16[512,1024]{1,0:T(8,128)(2,1)S(1)}, bf16[512,1024]{1,0:T(8,128)(2,1)}, u32[]{:S(2)}) copy-start(bf16[512,1024]{1,0:T(8,128)(2,1)} %get-tuple-element.24.item_ref) | copy-start | bytes 3145732
  97.5 22.1 %all-to-all-start.3 = ((f32[16,8,128]{2,1,0:T(8,128)}), f32[16,8,128]{2,1,0:T(8,128)S(1)}, u32[]{:S(2)}, u32[]{:S(2)}) async-start(f32[16,8,128]{2,1,0:T(8,128)} %get-tuple-element.17), calls=%async_computation.3 | async-start | bytes 131072 | tf_op jit(solution)/shard_map/sums/all_to_all | solution.py:516
  108.1 1.2 %copy-start.1 = (bf16[128,4096]{1,0:T(8,128)(2,1)S(1)}, bf16[128,4096]{1,0:T(8,128)(2,1)}, u32[]{:S(2)}) copy-start(bf16[128,4096]{1,0:T(8,128)(2,1)} %get-tuple-element.18.pre_ref) | copy-start | bytes 3145732
  109.3 1.0 copy-start.2
  110.3 1.0 copy-start.3

commit v2 on v1

--- a/solution.py
+++ b/solution.py
@@ -181,9 +181,9 @@
 def forward_kernel(
     order_ref, segments_ref, got_ref, near_in, far_in, negatives_ref, targets_ref, ratios_ref,
     topk_ref,
-    grad_ref, invd_ref, inv_ref, ditem_out, user_out, item_out, pre_out, normed_out,
-    pre_ref, normed_ref, resid_ref, ditem_ref, user_ref, item_ref, weight_ref, near_ref, far_ref,
-    in_sems, out_sems,
+    invd_ref, inv_ref, pair_out, sums_out, user_out, item_out, pre_out, normed_out,
+    pre_ref, normed_ref, resid_ref, pair_ref, sums_ref, user_ref, item_ref, weight_ref, near_ref,
+    far_ref, in_sems, out_sems,
 ):
     slots = got_ref.shape[0]
     rows, width = normed_ref.shape
@@ -203,7 +203,7 @@
         columns = slice(part * width, (part + 1) * width)
         pre_ref[:, columns] = dot_nn(pick, got_ref[:, columns]).astype(BF)
     resid_ref[...] = dot_nn(pick, got_ref[:, 4 * width :])
-    save_pre = pltpu.make_async_copy(pre_ref, pre_out, out_sems.at[6])
+    save_pre = pltpu.make_async_copy(pre_ref, pre_out, out_sems.at[2])
     save_pre.start()
     mask = causal_mask(segments_ref[...])
     scaling = head ** (-0.5)
@@ -225,7 +225,7 @@
     inv_dev = lax.rsqrt(jnp.mean(centered * centered, 1, keepdims=True) + 1e-05)
     normed = centered * inv_dev
     normed_ref[...] = normed
-    save_normed = pltpu.make_async_copy(normed_ref, normed_out, out_sems.at[7])
+    save_normed = pltpu.make_async_copy(normed_ref, normed_out, out_sems.at[3])
     save_normed.start()
     invd_ref[...] = inv_dev
     gate = pre_ref[:, :width].astype(F32)
@@ -274,29 +274,21 @@
     ratio = as_column(ratios_ref[...])
     row_weight = ratio * (size.astype(F32) * power)
     grad = (SHARP * row_weight) * (mass / totals - onehot)
-    grad_bf = grad.astype(BF)
-    grad_ref[...] = grad_bf
+    pair_ref[:, :items] = grad.astype(BF)
+    pair_ref[:, items:] = user_bf
+    save_pair = pltpu.make_async_copy(pair_ref, pair_out, out_sems.at[5])
+    save_pair.start()
     numerator = jnp.sum(row_weight * row_loss, 0, keepdims=True)
-    lanes = lax.broadcasted_iota(jnp.int32, (items, 128), 1)
-    extra = jnp.zeros((items, 128), F32)
-    pieces = in_pieces(numerator) + in_pieces(jnp.sum(ratio, 0, keepdims=True))
-    for lane, piece in enumerate(pieces):
-        extra = jnp.where(lanes == lane, piece, extra)
-    ditem_ref[:, width:] = extra.astype(BF)
-    out = []
-    steps = 4
-    for step in range(steps):
-        at = slice(step * items // steps, (step + 1) * items // steps)
-        ditem_ref[at, :width] = dot_tn(grad_bf[:, at], user_bf).astype(BF)
-        out.append(
-            pltpu.make_async_copy(ditem_ref.at[at, :], ditem_out.at[at, :], out_sems.at[2 + step])
-        )
-        out[-1].start()
-    for copy in [save_user, save_item, save_pre, save_normed] + out:
+    lanes = lax.broadcasted_iota(jnp.int32, sums_ref.shape[1:], 1)
+    both = jnp.where(lanes == 0, numerator, jnp.sum(ratio, 0, keepdims=True))
+    sums_ref[...] = jnp.broadcast_to(both[None], sums_ref.shape)
+    save_sums = pltpu.make_async_copy(sums_ref, sums_out, out_sems.at[4])
+    save_sums.start()
+    for copy in [save_user, save_item, save_pre, save_normed, save_sums, save_pair]:
         copy.wait()
 
 
-def forward_pass(order, segments, got, near, far, negatives, targets, ratios, topk):
+def forward_pass(order, segments, got, near, far, negatives, targets, ratios, topk, copies):
     rows = order.shape[1]
     width = got.shape[1] // 5
     members, block = near.shape[:2]
@@ -304,12 +296,12 @@
     return pl.pallas_call(
         forward_kernel,
         in_specs=vmem(3) + hbm(2) + vmem(3) + [pl.BlockSpec(memory_space=pltpu.SMEM)],
-        out_specs=vmem(3) + hbm(5),
+        out_specs=vmem(2) + hbm(6),
         out_shape=[
-            jax.ShapeDtypeStruct((rows, items), BF),
             jax.ShapeDtypeStruct((rows, 1), F32),
             jax.ShapeDtypeStruct((rows, 1), F32),
-            pltpu.HBM((items, width + 128), BF),
+            pltpu.HBM((rows, items + width), BF),
+            pltpu.HBM((copies, 8, 128), F32),
             pltpu.HBM((rows, width), F32),
             pltpu.HBM((items, width), BF),
             pltpu.HBM((rows, 4 * width), BF),
@@ -319,36 +311,130 @@
             pltpu.VMEM((rows, 4 * width), BF),
             pltpu.VMEM((rows, width), F32),
             pltpu.VMEM((rows, width), F32),
-            pltpu.VMEM((items, width + 128), BF),
+            pltpu.VMEM((rows, items + width), BF),
+            pltpu.VMEM((copies, 8, 128), F32),
             pltpu.VMEM((rows, width), F32),
             pltpu.VMEM((items, width), BF),
             pltpu.VMEM((members, 2, block, width), BF),
             pltpu.VMEM((members, block, width // 2), BF),
             pltpu.VMEM((members, block, width // 2), BF),
             pltpu.SemaphoreType.DMA((2 * PLANES + 2,)),
-            pltpu.SemaphoreType.DMA((8,)),
+            pltpu.SemaphoreType.DMA((6,)),
         ],
         compiler_params=pltpu.CompilerParams(**PARAMS),
-        cost_estimate=estimate(2 * rows * width * 3328, 12 * 1024 * 1024),
+        cost_estimate=estimate(2 * rows * width * 2816, 12 * 1024 * 1024),
         name="forward_pass",
     )(order, segments, got, *in_hbm(near, far), negatives, targets, ratios, topk)
 
 
+def items_kernel(own_in, other_ref, out_ref, own_ref, ditem_ref, in_sem, out_sem):
+    load = pltpu.make_async_copy(own_in, own_ref, in_sem)
+    load.start()
+    chips, _, block, width = ditem_ref.shape
+    items = chips * 2 * block
+    core = lax.axis_index("c")
+    load.wait()
+    users = jnp.concatenate([own_ref[:, items:], other_ref[:, items:]], 0)
+    grads = jnp.concatenate([own_ref[:, :items], other_ref[:, :items]], 0)
+    steps = 4
+    part = chips // steps
+    for step in range(steps):
+        at = slice(step * part, (step + 1) * part)
+        some = grads[:, step * items // steps : (step + 1) * items // steps]
+        ditem_ref[at] = dot_tn(some, users).astype(BF).reshape(part, 2, block, width)
+    back = pltpu.make_async_copy(ditem_ref.at[:, core], out_ref, out_sem)
+    back.start()
+    back.wait()
+
+
+def items_pass(own, other, chips, items):
+    rows, columns = own.shape
+    width = columns - items
+    block = items // (2 * chips)
+    return pl.pallas_call(
+        items_kernel,
+        in_specs=hbm(1) + vmem(1),
+        out_specs=vmem(1)[0],
+        out_shape=jax.ShapeDtypeStruct((chips, block, width), BF),
+        scratch_shapes=[
+            pltpu.VMEM((rows, columns), BF),
+            pltpu.VMEM((chips, 2, block, width), BF),
+            pltpu.SemaphoreType.DMA,
+            pltpu.SemaphoreType.DMA,
+        ],
+        compiler_params=pltpu.CompilerParams(**PARAMS),
+        cost_estimate=estimate(4 * rows * items * width, 4 * 1024 * 1024),
+        name="items_pass",
+    )(*in_hbm(own), other)
+
+
+def join_kernel(ditem_ref, sums_ref, inv_ref, out_ref, same_ref, extra_ref, sems):
+    chips, block, width = ditem_ref.shape
+    first = pltpu.make_async_copy(ditem_ref, out_ref.at[:, :, :width], sems.at[0])
+    first.start()
+    same_ref[...] = inv_ref[...]
+    row = jnp.sum(sums_ref[...], 0)[:1]
+    lanes = lax.broadcasted_iota(jnp.int32, row.shape, 1)
+    numerator = jnp.sum(jnp.where(lanes == 0, row, 0.0), 1, keepdims=True)
+    total = jnp.sum(jnp.where(lanes == 1, row, 0.0), 1, keepdims=True)
+    places = lax.broadcasted_iota(jnp.int32, (block, 128), 1)
+    extra = jnp.zeros((block, 128), F32)
+    for lane, piece in enumerate(in_pieces(numerator) + in_pieces(total)):
+        extra = jnp.where(places == lane, piece, extra)
+    extra_ref[...] = jnp.broadcast_to(extra.astype(BF)[None], extra_ref.shape)
+    second = pltpu.make_async_copy(extra_ref, out_ref.at[:, :, width:], sems.at[1])
+    second.start()
+    first.wait()
+    second.wait()
+
+
+def join(d_item, sums, inv):
+    chips, block, width = d_item.shape
+    return pl.pallas_call(
+        join_kernel,
+        in_specs=vmem(3),
+        out_specs=hbm(1) + vmem(1),
+        out_shape=[
+            pltpu.HBM((chips, block, width + 128), BF),
+            jax.ShapeDtypeStruct(inv.shape, F32),
+        ],
+        scratch_shapes=[
+            pltpu.VMEM((chips, block, 128), BF),
+            pltpu.SemaphoreType.DMA((2,)),
+        ],
+        compiler_params=pltpu.CompilerParams(**PARAMS),
+        cost_estimate=estimate(d_item.size, 4 * d_item.size),
+        name="join",
+    )(d_item, sums, inv)
+
+
 def back_kernel(
-    pre_ref, normed_ref, invd_ref, segments_ref, grad_ref, user_ref, invo_ref, item_ref, near_in, far_in,
-    out_ref, weight_ref, sems,
+    invd_ref, segments_ref, invo_ref, pair_in, item_in, user_in, near_in, far_in, normed_in, pre_in,
+    out_ref,
+    grad_ref, item_ref, user_ref, weight_ref, normed_ref, pre_ref, sems, weight_sems,
 ):
     rows, width = normed_ref.shape
+    items = item_ref.shape[0]
     head = width // HEADS
-    into = weight_copies(near_in, far_in, weight_ref, sems)
-    for copy in into:
+    loads = [
+        (pair_in.at[:, :items], grad_ref), (item_in, item_ref), (user_in, user_ref),
+        (normed_in, normed_ref), (pre_in, pre_ref),
+    ]
+    loads = [pltpu.make_async_copy(p, q, sems.at[n]) for n, (p, q) in enumerate(loads)]
+    into = weight_copies(near_in, far_in, weight_ref, weight_sems)
+    for copy in loads[:3] + into + loads[3:]:
         copy.start()
+    mask = causal_mask(segments_ref[...])
+    for copy in loads[:3]:
+        copy.wait()
     user = user_ref[...]
     d_user = dot_nn(grad_ref[...], item_ref[...])
     d_output = invo_ref[...] * (d_user - user * jnp.sum(user * d_user, 1, keepdims=True))
     for copy in into:
         copy.wait()
     d_gated = dot_nt(d_output.astype(BF), weight_ref[...].reshape(width, width))
+    loads[3].wait()
+    loads[4].wait()
     normed = normed_ref[...]
     gate = pre_ref[:, :width].astype(F32)
     gate_s = sigmoid(gate)
@@ -361,7 +447,6 @@
         - normed * jnp.mean(d_normed * normed, 1, keepdims=True)
     )
     dmix_bf = d_mixed.astype(BF)
-    mask = causal_mask(segments_ref[...])
     scaling = head ** (-0.5)
 
     def opened(part, h):
@@ -393,89 +478,81 @@
             out_ref[:, start : start + head] = grad * rate
 
 
-def back_pass(pre, normed, inv_dev, segments, grad, user, inv_out, item, near, far):
+def back_pass(inv_dev, segments, inv_out, pair, item, user, near, far, normed, pre):
     rows, width = normed.shape
+    items = item.shape[0]
     members, block = near.shape[:2]
     return pl.pallas_call(
         back_kernel,
-        in_specs=vmem(8) + hbm(2),
-        out_specs=pl.BlockSpec(memory_space=pltpu.VMEM),
+        in_specs=vmem(3) + hbm(7),
+        out_specs=vmem(1)[0],
         out_shape=jax.ShapeDtypeStruct((rows, 4 * width), F32),
         scratch_shapes=[
+            pltpu.VMEM((rows, items), BF),
+            pltpu.VMEM((items, width), BF),
+            pltpu.VMEM((rows, width), F32),
             pltpu.VMEM((members, 2, block, width), BF),
+            pltpu.VMEM((rows, width), F32),
+            pltpu.VMEM((rows, 4 * width), BF),
+            pltpu.SemaphoreType.DMA((5,)),
             pltpu.SemaphoreType.DMA((2 * PLANES,)),
         ],
         compiler_params=pltpu.CompilerParams(**PARAMS),
         cost_estimate=estimate(2 * rows * width * 2304, 8 * 1024 * 1024),
         name="back_pass",
-    )(pre, normed, inv_dev, segments, grad, user, inv_out, item, *in_hbm(near, far))
-
-
-def table_kernel(got_ref, table_ref, out_ref, sums_ref):
+    )(inv_dev, segments, inv_out, *in_hbm(pair, item, user, near, far, normed, pre))
+
+
+def finish_kernel(
+    got_ref, table_ref, act_ref, loss_ref, proj_out, table_out, proj_ref, dtable_ref, sems
+):
     width = table_ref.shape[1]
+    row = jnp.sum(got_ref[:, :, width:].astype(F32), 0)[:1]
+    lanes = lax.broadcasted_iota(jnp.int32, row.shape, 1)
+    numerator = jnp.sum(jnp.where(lanes < 3, row, 0.0), 1, keepdims=True)
+    total = jnp.sum(jnp.where(lanes < 3, 0.0, row), 1, keepdims=True)
+    share = 1.0 / total
+    steps = sems.shape[0] - 1
+    size = act_ref.shape[0] // steps
+    out = []
+    for step in range(steps):
+        at = slice(step * size, (step + 1) * size)
+        proj_ref[at, :] = (act_ref[at, :] * share).astype(BF)
+        out.append(pltpu.make_async_copy(proj_ref.at[at, :], proj_out.at[at, :], sems.at[step]))
+        out[-1].start()
+    loss_ref[...] = jnp.broadcast_to(numerator * share, loss_ref.shape)
     summed = jnp.sum(got_ref[:, :, :width].astype(F32), 0)
     own = table_ref[...].astype(F32)
     inverse = lax.rsqrt(jnp.sum(own * own, 1, keepdims=True) + 1e-06)
     item = own * inverse
     inner = jnp.sum(item * summed, 1, keepdims=True)
-    out_ref[...] = inverse * (summed - item * inner)
-    extra = jnp.sum(got_ref[:, :, width:].astype(F32), 0)[:8]
-    sums_ref[...] = jnp.broadcast_to(extra[None], sums_ref.shape)
-
-
-def table_pass(got, table, groups):
-    return pl.pallas_call(
-        table_kernel,
-        in_specs=vmem(2),
-        out_specs=vmem(2),
-        out_shape=[
-            jax.ShapeDtypeStruct(table.shape, F32),
-            jax.ShapeDtypeStruct((groups, 8, 128), F32),
-        ],
-        compiler_params=pltpu.CompilerParams(**PARAMS),
-        cost_estimate=estimate(got.size * 2, got.size * 2),
-        name="table_pass",
-    )(got, table)
-
-
-def finish_kernel(sums_ref, act_ref, table_ref, loss_ref, proj_out, out_ref, proj_ref, sems):
-    row = jnp.sum(sums_ref[...], 0)[:1]
-    lanes = lax.broadcasted_iota(jnp.int32, row.shape, 1)
-    numerator = jnp.sum(jnp.where(lanes < 3, row, 0.0), 1, keepdims=True)
-    total = jnp.sum(jnp.where(lanes < 3, 0.0, row), 1, keepdims=True)
-    share = 1.0 / total
-    steps = 4
-    size = act_ref.shape[0] // steps
-    out = []
-    for step in range(steps):
-        at = slice(step * size, (step + 1) * size)
-        proj_ref[at, :] = (act_ref[at, :] * share).astype(BF)
-        out.append(
-            pltpu.make_async_copy(proj_ref.at[at, :], proj_out.at[at, :], sems.at[step])
-        )
-        out[-1].start()
-    loss_ref[...] = jnp.broadcast_to(numerator * share, loss_ref.shape)
-    out_ref[...] = table_ref[...] * share
+    dtable_ref[...] = (share * inverse) * (summed - item * inner)
+    out.append(pltpu.make_async_copy(dtable_ref, table_out, sems.at[steps]))
+    out[-1].start()
     for copy in out:
         copy.wait()
 
 
-def finish(sums, d_act, d_table):
+def finish(got, table, d_act):
     rows, columns = d_act.shape
     return pl.pallas_call(
         finish_kernel,
         in_specs=vmem(3),
-        out_specs=vmem(1) + hbm(1) + vmem(1),
+        out_specs=vmem(1) + hbm(2),
         out_shape=[
             jax.ShapeDtypeStruct((1, 128), F32),
-            jax.ShapeDtypeStruct((rows, columns), BF),
-            jax.ShapeDtypeStruct(d_table.shape, F32),
-        ],
-        scratch_shapes=[pltpu.VMEM((rows, columns), BF), pltpu.SemaphoreType.DMA((4,))],
+            pltpu.HBM((rows, columns), BF),
+            pltpu.HBM(table.shape, F32),
+        ],
+        scratch_shapes=[
+            pltpu.VMEM((rows, columns), BF),
+            pltpu.VMEM(table.shape, F32),
+            pltpu.SemaphoreType.DMA((5,)),
+        ],
         compiler_params=pltpu.CompilerParams(**PARAMS),
         cost_estimate=estimate(rows * columns, rows * columns * 6),
         name="finish",
-    )(sums, d_act, d_table)
+    )(got, table, d_act)
 
 
 def shards(
@@ -503,18 +580,18 @@
             parts.append(lax.ppermute(mine_part, "z", pairs))
         near = jnp.concatenate(parts + [share[:, :, size:]], 2)
         far = lax.ppermute(near, "c", [(0, 1), (1, 0)])
-    grad, inv_dev, inv_out, d_item, user, item, pre, normed = forward_pass(
-        pack_rows, segments, got, near, far, negatives, targets, ratios, topk
+    inv_dev, inv_out, pair, sums, user, item, pre, normed = forward_pass(
+        pack_rows, segments, got, near, far, negatives, targets, ratios, topk, 2 * groups
     )
+    with jax.named_scope("sums"):
+        sums = lax.all_to_all(sums, ("z", "c"), 0, 0, tiled=True)
     with jax.named_scope("items_back"):
-        got_item = lax.all_to_all(
-            d_item.reshape(members, mine, width + 128), MEMBERS, 0, 0, tiled=True
-        )
-    d_act = back_pass(pre, normed, inv_dev, segments, grad, user, inv_out, item, near, far)
-    d_table, sums = table_pass(got_item, table, groups)
-    with jax.named_scope("sums"):
-        sums = lax.all_to_all(sums, "z", 0, 0, tiled=True)
-    loss, d_proj, d_table = finish(sums, d_act, d_table)
+        pair_other = lax.ppermute(pair, "c", [(0, 1), (1, 0)])
+        d_item = items_pass(pair, pair_other, members // 2, members * mine)
+        d_item, inv_out = join(d_item, sums, inv_out)
+        got_item = lax.all_to_all(d_item, ("x", "y"), 0, 0, tiled=True)
+    d_act = back_pass(inv_dev, segments, inv_out, pair, item, user, near, far, normed, pre)
+    loss, d_proj, d_table = finish(got_item, table, d_act)
     return (loss[0, :1], d_proj, d_table)
 
 

time: 122 us -> 117 us (0.959)
  blocking collectives: 26.3 us -> 0 us
  waiting for transfers between devices: 25.8 us -> 38.1 us
  starting transfers between devices: 42.9 us -> 52.4 us
  local copies, waits for them, and re-layouts: 7.34 us -> 4.08 us
  Pallas kernels: 17.6 us -> 19.1 us
    all_to_all x1 -> x0, blocking collectives: 26.3 us -> none  [shards(): lax.all_to_all(d_item.reshape(members, mine, width + 128), MEMBERS, 0, 0,...]
    all_to_all x1 -> x2, waiting for transfers between devices: 3.8 us -> 14.5 us  [the longest x1 10.5 us: shards(): sums = lax.all_to_all(sums, ('z', 'c'), 0, 0, tiled=True)]
    all_to_all x1 -> x2, starting transfers between devices: 10.5 us -> 17.9 us  [the longest x1 14.3 us: shards(): sums = lax.all_to_all(sums, ('z', 'c'), 0, 0, tiled=True)]
    unnamed x23 -> x15, local copies, waits for them, and re-layouts: 5.64 us -> 2.39 us
    pallas_call x3 -> x4, Pallas kernels: 7.07 us -> 9.32 us  [the longest x1 5.25 us: back_pass(): pl.pallas_call(back_kernel, in_specs=vmem(3) + hbm(7), out_specs=vmem(1)[...]
    ppermute x0 -> x1, starting transfers between devices: none -> 2.14 us  [shards(): pair_other = lax.ppermute(pair, 'c', [(0, 1), (1, 0)])]
    ppermute x0 -> x1, waiting for transfers between devices: none -> 1.67 us  [shards(): pair_other = lax.ppermute(pair, 'c', [(0, 1), (1, 0)])]
  transfers between devices with their start and end apart: 7 -> 9, of which waited for: 5 -> 7; matrix products, arithmetic and copies ran while one was open for 3% -> 4% of each run, Pallas kernels for 6% -> 9%
where the time goes in v2:
time: 117 us; the launch traced here: 115 us
  starting transfers between devices  52.4 us (45%)
  waiting for transfers between devices  38.1 us (33%)
  Pallas kernels  19.1 us (16%)
  local copies, waits for them, and re-layouts  4.08 us (3%)
  between operations  1.49 us (1%)
    ppermute x3, starting transfers between devices, shards(): parts.append(lax.ppermute(mine_part, 'z', pairs))  14.9 us
    all_to_all x1, starting transfers between devices, shards(): sums = lax.all_to_all(sums, ('z', 'c'), 0, 0, tiled=True)  14.3 us
    all_to_all x1, waiting for transfers between devices, shards(): lax.all_to_all(share.reshape(members, mine, share.shape[1]), MEMBERS, 0,...  11 us
    all_to_all x1, waiting for transfers between devices, shards(): sums = lax.all_to_all(sums, ('z', 'c'), 0, 0, tiled=True)  10.5 us
    all_to_all x1, starting transfers between devices, shards(): lax.all_to_all(share.reshape(members, mine, share.shape[1]), MEMBERS, 0,...  10.5 us
    ppermute x3, waiting for transfers between devices, shards(): parts.append(lax.ppermute(mine_part, 'z', pairs))  8.07 us
    pallas_call x1, Pallas kernels, back_pass(): pl.pallas_call(back_kernel, in_specs=vmem(3) + hbm(7), out_specs=vmem(1)[...  5.25 us
    pallas_call x1, Pallas kernels, forward_pass(): pl.pallas_call(forward_kernel, in_specs=vmem(3) + hbm(2) + vmem(3) + [pl....  4.66 us
  transfers between devices with their start and end apart: 9, of which 7 were waited for; matrix products, arithmetic and copies ran while one was open for 4% of the time, Pallas kernels for 9%

profile of v2, /device:TPU:1, one launch (start us, length us, event | category | flops | bytes accessed | tf_op | source)
XLA Modules:
  0.0 115.2 jit_solution(13315153894317403571)
XLA Ops:
  0.6 1.8 %shared_blocks.1 = bf16[512,768]{1,0:T(8,128)(2,1)} custom-call(bf16[16,1024]{1,0:T(8,128)(2,1)} %table_ref.1, bf16[32,1024]{1,0:T(8,128)(2,1)} %weight_in.1), custom_call_target="tpu_custom_call" | custom-call | flops 786432 | bytes 786432 | tf_op jit(solution)/shard_map/shared/shared_blocks/pallas_call | solution.py:132
  2.4 10.5 %all-to-all-start.1 = ((bf16[32,16,768]{2,1,0:T(8,128)(2,1)}), bf16[32,16,768]{2,1,0:T(8,128)(2,1)S(1)}, u32[]{:S(2)}, u32[]{:S(2)}) async-start(bf16[32,16,768]{2,1,0:T(8,128)(2,1)} %bitcast.7), calls=%async_computation.1 | async-start | bytes 1572864 | tf_op jit(solution)/shard_map/shared/all_to_all | solution.py:566
  12.9 3.3 %send_blocks.1 = bf16[256,5120]{1,0:T(8,128)(2,1)} custom-call(s32[1,256]{1,0:T(1,128)} %slots_in.1, bf16[128,4096]{1,0:T(8,128)(2,1)} %proj_in.1, bf16[128,1024]{1,0:T(8,128)(2,1)} %resid_in.1), custom_call_target="tpu_custom_call" | custom-call | flops 335544320 | bytes 3932160 | tf_op jit(solution)/shard_map/route/send_blocks/pallas_call | solution.py:83
  16.2 11.0 %all-to-all-done.1 = bf16[32,16,768]{2,1,0:T(8,128)(2,1)S(1)} async-done(((bf16[32,16,768]{2,1,0:T(8,128)(2,1)}), bf16[32,16,768]{2,1,0:T(8,128)(2,1)S(1)}, u32[]{:S(2)}, u32[]{:S(2)}) %all-to-all-start.1) | async-done | bytes 786464 | tf_op jit(solution)/shard_map/shared/all_to_all | solution.py:566
  27.2 3.8 %all-to-all-start = ((bf16[32,8,5120]{2,1,0:T(8,128)(2,1)}), bf16[32,8,5120]{2,1,0:T(8,128)(2,1)S(1)}, u32[]{:S(2)}, u32[]{:S(2)}) async-start(bf16[32,8,5120]{2,1,0:T(8,128)(2,1)} %bitcast.6), calls=%async_computation | async-start | bytes 5242880 | tf_op jit(solution)/shard_map/route/all_to_all | solution.py:571
  31.1 0.0 copy-start.1
  31.1 0.0 copy-start.2
  31.1 0.0 copy-start.3
  31.1 0.0 copy-start.4
  31.1 0.0 copy-start.5
  31.1 0.8 fusion
  31.9 9.1 %collective-permute-start = (bf16[32,16,256]{2,1,0:T(8,128)(2,1)S(1)}, bf16[32,16,256]{2,1,0:T(8,128)(2,1)S(1)}, u32[]{:S(2)}, u32[]{:S(2)}) collective-permute-start(bf16[32,16,256]{2,1,0:T(8,128)(2,1)S(1)} %get-tuple-element.29), channel_id=1, source_target_pairs={{0,480},{32,0},{64,32},{96,64},{128,96},{160,128},{192,160},{224,1... | collective-permute-start | bytes 786440 | tf_op jit(solution)/shard_map/planes/ppermute | solution.py:580
  41.1 1.9 %collective-permute-start.1 = (bf16[32,16,256]{2,1,0:T(8,128)(2,1)S(1)}, bf16[32,16,256]{2,1,0:T(8,128)(2,1)S(1)}, u32[]{:S(2)}, u32[]{:S(2)}) collective-permute-start(bf16[32,16,256]{2,1,0:T(8,128)(2,1)S(1)} %get-tuple-element.29), channel_id=1, source_target_pairs={{0,32},{32,64},{64,96},{96,128},{128,160},{160,192},{192,224},{224... | collective-permute-start | bytes 786440 | tf_op jit(solution)/shard_map/planes/ppermute | solution.py:580
  43.0 3.8 %collective-permute-start.2 = (bf16[32,16,256]{2,1,0:T(8,128)(2,1)S(1)}, bf16[32,16,256]{2,1,0:T(8,128)(2,1)S(1)}, u32[]{:S(2)}, u32[]{:S(2)}) collective-permute-start(bf16[32,16,256]{2,1,0:T(8,128)(2,1)S(1)} %get-tuple-element.29), channel_id=1, source_target_pairs={{0,448},{32,480},{64,0},{96,32},{128,64},{160,96},{192,128},{224,1... | collective-permute-start | bytes 786440 | tf_op jit(solution)/shard_map/planes/ppermute | solution.py:580
  46.8 0.0 collective-permute-done
  46.8 0.8 constant_dynamic-update-slice_fusion.2
  47.6 3.9 %collective-permute-done.1 = bf16[32,16,256]{2,1,0:T(8,128)(2,1)S(1)} collective-permute-done((bf16[32,16,256]{2,1,0:T(8,128)(2,1)S(1)}, bf16[32,16,256]{2,1,0:T(8,128)(2,1)S(1)}, u32[]{:S(2)}, u32[]{:S(2)}) %collective-permute-start.1) | collective-permute-done | bytes 262176 | tf_op jit(solution)/shard_map/planes/ppermute | solution.py:580
  51.5 0.8 constant_dynamic-update-slice_fusion.1
  52.3 4.1 %collective-permute-done.2 = bf16[32,16,256]{2,1,0:T(8,128)(2,1)S(1)} collective-permute-done((bf16[32,16,256]{2,1,0:T(8,128)(2,1)S(1)}, bf16[32,16,256]{2,1,0:T(8,128)(2,1)S(1)}, u32[]{:S(2)}, u32[]{:S(2)}) %collective-permute-start.2) | collective-permute-done | bytes 262176 | tf_op jit(solution)/shard_map/planes/ppermute | solution.py:580
  56.4 0.8 constant_dynamic-update-slice_fusion
  57.2 0.9 slice_dynamic-update-slice_fusion.near_in
  58.1 3.2 %collective-permute-start.3 = (bf16[32,16,1536]{2,1,0:T(8,128)(2,1)}, bf16[32,16,1536]{2,1,0:T(8,128)(2,1)}, u32[]{:S(2)}, u32[]{:S(2)}) collective-permute-start(bf16[32,16,1536]{2,1,0:T(8,128)(2,1)} %slice_dynamic-update-slice_fusion.near_in), channel_id=1, source_target_pairs={{0,1},{1,0},{2,3},{3,2},{4,5},{5,4},{6,7},{7,6},{8,9},{9,8},{10,11... | collective-permute-start | bytes 4718600 | tf_op jit(solution)/shard_map/planes/ppermute | solution.py:582
  62.0 2.9 %all-to-all-done = bf16[32,8,5120]{2,1,0:T(8,128)(2,1)S(1)} async-done(((bf16[32,8,5120]{2,1,0:T(8,128)(2,1)}), bf16[32,8,5120]{2,1,0:T(8,128)(2,1)S(1)}, u32[]{:S(2)}, u32[]{:S(2)}) %all-to-all-start) | async-done | bytes 2621472 | tf_op jit(solution)/shard_map/route/all_to_all | solution.py:571
  64.9 0.0 collective-permute-done.3.far_in
  64.9 0.0 copy-done.1
  64.9 0.0 copy-done.2
  64.9 0.0 copy-done.3
  64.9 0.0 copy-done.4
  64.9 0.0 copy-done.5
  64.9 4.7 %forward_pass.1 = (f32[128,1]{1,0:T(8,128)S(1)}, f32[128,1]{1,0:T(8,128)S(1)}, bf16[128,1536]{1,0:T(8,128)(2,1)}, f32[32,8,128]{2,1,0:T(8,128)}, f32[128,1024]{1...) custom-call(s32[1,128]{1,0:T(1,128)S(1)} %copy-done.3, ...), custom_call_target="tpu_custom_call" | custom-call | flops 738197504 | bytes 12582912 | tf_op jit(solution)/shard_map/forward_pass/pallas_call | solution.py:296
  69.6 14.3 %all-to-all-start.2 = ((f32[32,8,128]{2,1,0:T(8,128)}), f32[32,8,128]{2,1,0:T(8,128)S(1)}, u32[]{:S(2)}, u32[]{:S(2)}) async-start(f32[32,8,128]{2,1,0:T(8,128)} %get-tuple-element.17), calls=%async_computation.2 | async-start | bytes 262144 | tf_op jit(solution)/shard_map/sums/all_to_all | solution.py:587
  83.9 2.1 %collective-permute-start.4 = (bf16[128,1536]{1,0:T(8,128)(2,1)}, bf16[128,1536]{1,0:T(8,128)(2,1)S(1)}, u32[]{:S(2)}, u32[]{:S(2)}) collective-permute-start(bf16[128,1536]{1,0:T(8,128)(2,1)} %get-tuple-element.16.own_in.pair_in), channel_id=1, source_target_pairs={{0,1},{1,0},{2,3},{3,2},{4,5},{5,4},{6,7},{7,6},{8,9},{9,8},{10,11... | collective-permute-start | bytes 1179656 | tf_op jit(solution)/shard_map/items_back/ppermute | solution.py:589
  86.1 1.7 %collective-permute-done.4.other_ref = bf16[128,1536]{1,0:T(8,128)(2,1)S(1)} collective-permute-done((bf16[128,1536]{1,0:T(8,128)(2,1)}, bf16[128,1536]{1,0:T(8,128)(2,1)S(1)}, u32[]{:S(2)}, u32[]{:S(2)}) %collective-permute-start.4) | collective-permute-done | bytes 393248 | tf_op jit(solution)/shard_map/items_back/ppermute | solution.py:589
  87.8 1.5 %items_pass.1.ditem_ref = bf16[16,16,1024]{2,1,0:T(8,128)(2,1)S(1)} custom-call(bf16[128,1536]{1,0:T(8,128)(2,1)} %get-tuple-element.16.own_in.pair_in, bf16[128,1536]{1,0:T(8,128)(2,1)S(1)} %collective-permute-done.4.other_ref), custom_call_target="tpu_custom_call" | custom-call | flops 268435456 | bytes 4194304 | tf_op jit(solution)/shard_map/items_back/items_pass/pallas_call | solution.py:354
  89.3 10.5 %all-to-all-done.2.sums_ref = f32[32,8,128]{2,1,0:T(8,128)S(1)} async-done(((f32[32,8,128]{2,1,0:T(8,128)}), f32[32,8,128]{2,1,0:T(8,128)S(1)}, u32[]{:S(2)}, u32[]{:S(2)}) %all-to-all-start.2) | async-done | bytes 131104 | tf_op jit(solution)/shard_map/sums/all_to_all | solution.py:587
  99.8 0.9 join.1
  100.6 3.6 %all-to-all-start.3 = ((bf16[16,16,1152]{2,1,0:T(8,128)(2,1)}), bf16[16,16,1152]{2,1,0:T(8,128)(2,1)S(1)}, u32[]{:S(2)}, u32[]{:S(2)}) async-start(bf16[16,16,1152]{2,1,0:T(8,128)(2,1)} %get-tuple-element.19), calls=%async_computation.3 | async-start | bytes 1179648 | tf_op jit(solution)/shard_map/items_back/all_to_all | solution.py:592
  104.2 0.0 copy-start
  104.3 5.3 %back_pass.1.act_ref = f32[128,4096]{1,0:T(8,128)S(1)} custom-call(f32[128,1]{1,0:T(8,128)S(1)} %get-tuple-element.20.invd_ref, s32[1,128]{1,0:T(1,128)S(1)} %copy-done.1, f32[128,1]{1,0:T(8,128)S(1)} %get-tuple-element.21.invo_ref, bf16[128,1536]{1,0:T(8,128)(2,1)} %get-tuple-element.16.own_in.pair_in, bf16[512,1024]{1,0:T(8,128)(2,1)} %get-tuple-element.22.item_in, ...), custom_call_target="tpu_custom_call" | custom-call | flops 603979776 | bytes 8388608 | tf_op jit(solution)/shard_map/back_pass/pallas_call | solution.py:485
  109.5 4.0 %all-to-all-done.3.got_ref = bf16[16,16,1152]{2,1,0:T(8,128)(2,1)S(1)} async-done(((bf16[16,16,1152]{2,1,0:T(8,128)(2,1)}), bf16[16,16,1152]{2,1,0:T(8,128)(2,1)S(1)}, u32[]{:S(2)}, u32[]{:S(2)}) %all-to-all-start.3) | async-done | bytes 589856 | tf_op jit(solution)/shard_map/items_back/all_to_all | solution.py:592
  113.6 0.0 copy-done
  113.6 1.7 %finish.1 = (f32[1,128]{1,0:T(1,128)}, bf16[128,4096]{1,0:T(8,128)(2,1)}, f32[16,1024]{1,0:T(8,128)}) custom-call(bf16[16,16,1152]{2,1,0:T(8,128)(2,1)S(1)} %all-to-all-done.3.got_ref, bf16[16,1024]{1,0:T(8,128)(2,1)S(1)} %copy-done, f32[128,4096]{1,0:T(8,128)S(1)} %back_pass.1.act_ref), custom_call_target="tpu_custom_call" | custom-call | flops 524288 | bytes 3145728 | tf_op jit(solution)/shard_map/finish/pallas_call | solution.py:538
Async XLA Ops:
  2.4 24.8 %all-to-all-start.1 = ((bf16[32,16,768]{2,1,0:T(8,128)(2,1)}), bf16[32,16,768]{2,1,0:T(8,128)(2,1)S(1)}, u32[]{:S(2)}, u32[]{:S(2)}) async-start(bf16[32,16,768]{2,1,0:T(8,128)(2,1)} %bitcast.7), calls=%async_computation.1 | async-start | bytes 1572864 | tf_op jit(solution)/shard_map/shared/all_to_all | solution.py:566
  27.2 37.7 %all-to-all-start = ((bf16[32,8,5120]{2,1,0:T(8,128)(2,1)}), bf16[32,8,5120]{2,1,0:T(8,128)(2,1)S(1)}, u32[]{:S(2)}, u32[]{:S(2)}) async-start(bf16[32,8,5120]{2,1,0:T(8,128)(2,1)} %bitcast.6), calls=%async_computation | async-start | bytes 5242880 | tf_op jit(solution)/shard_map/route/all_to_all | solution.py:571
  31.1 33.8 %copy-start.1 = (s32[1,128]{1,0:T(1,128)S(1)}, s32[1,128]{1,0:T(1,128)}, u32[]{:S(2)}) copy-start(s32[1,128]{1,0:T(1,128)} %segments_ref.3) | copy-start | bytes 1540
  31.1 33.8 %copy-start.2 = (s32[1,256]{1,0:T(1,128)S(1)}, s32[1,256]{1,0:T(1,128)}, u32[]{:S(2)}) copy-start(s32[1,256]{1,0:T(1,128)} %negatives_ref.1) | copy-start | bytes 3076
  31.1 33.8 %copy-start.3 = (s32[1,128]{1,0:T(1,128)S(1)}, s32[1,128]{1,0:T(1,128)}, u32[]{:S(2)}) copy-start(s32[1,128]{1,0:T(1,128)} %order_ref.1) | copy-start | bytes 1540
  31.1 33.8 %copy-start.4 = (s32[1,128]{1,0:T(1,128)S(1)}, s32[1,128]{1,0:T(1,128)}, u32[]{:S(2)}) copy-start(s32[1,128]{1,0:T(1,128)} %targets_ref.1) | copy-start | bytes 1540
  31.1 33.8 %copy-start.5 = (f32[1,128]{1,0:T(1,128)S(1)}, f32[1,128]{1,0:T(1,128)}, u32[]{:S(2)}) copy-start(f32[1,128]{1,0:T(1,128)} %ratios_ref.1) | copy-start | bytes 1540
  31.9 14.9 %collective-permute-start = (bf16[32,16,256]{2,1,0:T(8,128)(2,1)S(1)}, bf16[32,16,256]{2,1,0:T(8,128)(2,1)S(1)}, u32[]{:S(2)}, u32[]{:S(2)}) collective-permute-start(bf16[32,16,256]{2,1,0:T(8,128)(2,1)S(1)} %get-tuple-element.29), channel_id=1, source_target_pairs={{0,480},{32,0},{64,32},{96,64},{128,96},{160,128},{192,160},{224,1... | collective-permute-start | bytes 786440 | tf_op jit(solution)/shard_map/planes/ppermute | solution.py:580
  41.1 10.5 %collective-permute-start.1 = (bf16[32,16,256]{2,1,0:T(8,128)(2,1)S(1)}, bf16[32,16,256]{2,1,0:T(8,128)(2,1)S(1)}, u32[]{:S(2)}, u32[]{:S(2)}) collective-permute-start(bf16[32,16,256]{2,1,0:T(8,128)(2,1)S(1)} %get-tuple-element.29), channel_id=1, source_target_pairs={{0,32},{32,64},{64,96},{96,128},{128,160},{160,192},{192,224},{224... | collective-permute-start | bytes 786440 | tf_op jit(solution)/shard_map/planes/ppermute | solution.py:580
  43.0 13.4 %collective-permute-start.2 = (bf16[32,16,256]{2,1,0:T(8,128)(2,1)S(1)}, bf16[32,16,256]{2,1,0:T(8,128)(2,1)S(1)}, u32[]{:S(2)}, u32[]{:S(2)}) collective-permute-start(bf16[32,16,256]{2,1,0:T(8,128)(2,1)S(1)} %get-tuple-element.29), channel_id=1, source_target_pairs={{0,448},{32,480},{64,0},{96,32},{128,64},{160,96},{192,128},{224,1... | collective-permute-start | bytes 786440 | tf_op jit(solution)/shard_map/planes/ppermute | solution.py:580
  58.1 6.8 %collective-permute-start.3 = (bf16[32,16,1536]{2,1,0:T(8,128)(2,1)}, bf16[32,16,1536]{2,1,0:T(8,128)(2,1)}, u32[]{:S(2)}, u32[]{:S(2)}) collective-permute-start(bf16[32,16,1536]{2,1,0:T(8,128)(2,1)} %slice_dynamic-update-slice_fusion.near_in), channel_id=1, source_target_pairs={{0,1},{1,0},{2,3},{3,2},{4,5},{5,4},{6,7},{7,6},{8,9},{9,8},{10,11... | collective-permute-start | bytes 4718600 | tf_op jit(solution)/shard_map/planes/ppermute | solution.py:582
  69.6 30.2 %all-to-all-start.2 = ((f32[32,8,128]{2,1,0:T(8,128)}), f32[32,8,128]{2,1,0:T(8,128)S(1)}, u32[]{:S(2)}, u32[]{:S(2)}) async-start(f32[32,8,128]{2,1,0:T(8,128)} %get-tuple-element.17), calls=%async_computation.2 | async-start | bytes 262144 | tf_op jit(solution)/shard_map/sums/all_to_all | solution.py:587
  83.9 3.8 %collective-permute-start.4 = (bf16[128,1536]{1,0:T(8,128)(2,1)}, bf16[128,1536]{1,0:T(8,128)(2,1)S(1)}, u32[]{:S(2)}, u32[]{:S(2)}) collective-permute-start(bf16[128,1536]{1,0:T(8,128)(2,1)} %get-tuple-element.16.own_in.pair_in), channel_id=1, source_target_pairs={{0,1},{1,0},{2,3},{3,2},{4,5},{5,4},{6,7},{7,6},{8,9},{9,8},{10,11... | collective-permute-start | bytes 1179656 | tf_op jit(solution)/shard_map/items_back/ppermute | solution.py:589
  100.6 12.9 %all-to-all-start.3 = ((bf16[16,16,1152]{2,1,0:T(8,128)(2,1)}), bf16[16,16,1152]{2,1,0:T(8,128)(2,1)S(1)}, u32[]{:S(2)}, u32[]{:S(2)}) async-start(bf16[16,16,1152]{2,1,0:T(8,128)(2,1)} %get-tuple-element.19), calls=%async_computation.3 | async-start | bytes 1179648 | tf_op jit(solution)/shard_map/items_back/all_to_all | solution.py:592
  104.2 9.3 %copy-start = (bf16[16,1024]{1,0:T(8,128)(2,1)S(1)}, bf16[16,1024]{1,0:T(8,128)(2,1)}, u32[]{:S(2)}) copy-start(bf16[16,1024]{1,0:T(8,128)(2,1)} %table_ref.1) | copy-start | bytes 98308

commit v3 on v2

--- a/solution.py
+++ b/solution.py
@@ -30,11 +30,6 @@
 
 def sigmoid(values):
     return 1.0 / (1.0 + jnp.exp(-values))
-
-
-def as_column(row):
-    n = row.shape[1]
-    return jnp.broadcast_to(row, (n, n)).T[:, :1]
 
 
 def vmem(count):
@@ -178,10 +173,23 @@
     return high, middle, value - high - middle
 
 
+def unit_items(near_ref, far_ref, items):
+    first = lax.axis_index("c") == 0
+    near = near_ref[...].astype(F32)
+    far = far_ref[...].astype(F32)
+    near = jnp.concatenate([near[:, :8], near[:, 8:]], 2)
+    far = jnp.concatenate([far[:, :8], far[:, 8:]], 2)
+    low = jnp.where(first, near, far)
+    high = jnp.where(first, far, near)
+    values = jnp.concatenate([low, high], 1).reshape(items, near.shape[2])
+    inverse = lax.rsqrt(jnp.sum(values * values, 1, keepdims=True) + 1e-06)
+    return (values * inverse).astype(BF)
+
+
 def forward_kernel(
     order_ref, segments_ref, got_ref, near_in, far_in, negatives_ref, targets_ref, ratios_ref,
     topk_ref,
-    invd_ref, inv_ref, pair_out, sums_out, user_out, item_out, pre_out, normed_out,
+    invd_ref, inv_ref, pair_out, sums_out, user_out, pre_out, normed_out,
     pre_ref, normed_ref, resid_ref, pair_ref, sums_ref, user_ref, item_ref, weight_ref, near_ref,
     far_ref, in_sems, out_sems,
 ):
@@ -241,28 +249,23 @@
     save_user.start()
     inv_ref[...] = inverse
     user_bf = user.astype(BF)
+    lane = 128
+    for n in range(width // lane):
+        pair_ref[items + n * rows : items + (n + 1) * rows, :] = user_bf[:, n * lane : (n + 1) * lane]
+    save_half = pltpu.make_async_copy(
+        pair_ref.at[items:, :], pair_out.at[items:, :], out_sems.at[1]
+    )
+    save_half.start()
+    item_ref[...] = unit_items(near_ref, far_ref, items)
     drawn = negatives_ref.shape[1]
     hits = (lax.broadcasted_iota(jnp.int32, (items, drawn), 0) == negatives_ref[...]).astype(F32)
-    counts = dot_nt(jnp.ones((8, drawn), BF), hits.astype(BF))[:1]
-    ids = lax.broadcasted_iota(jnp.int32, (rows, items), 1)
-    target = as_column(targets_ref[...].astype(F32)).astype(jnp.int32)
-    onehot = jnp.where(ids == target, 1.0, 0.0)
-    first = lax.axis_index("c") == 0
-    near = near_ref[...].astype(F32)
-    far = far_ref[...].astype(F32)
-    near = jnp.concatenate([near[:, :8], near[:, 8:]], 2)
-    far = jnp.concatenate([far[:, :8], far[:, 8:]], 2)
-    low = jnp.where(first, near, far)
-    high = jnp.where(first, far, near)
-    values = jnp.concatenate([low, high], 1).reshape(items, width)
-    item_inv = lax.rsqrt(jnp.sum(values * values, 1, keepdims=True) + 1e-06)
-    item_ref[...] = (values * item_inv).astype(BF)
-    save_item = pltpu.make_async_copy(item_ref, item_out, out_sems.at[1])
-    save_item.start()
-    logits = SHARP * dot_nt(user_bf, item_ref[...])
+    counts = dot_nn(hits.astype(BF), jnp.ones((drawn, rows), BF))
+    ids = lax.broadcasted_iota(jnp.int32, (items, rows), 0)
+    onehot = jnp.where(ids == targets_ref[...], 1.0, 0.0)
+    logits = SHARP * dot_nt(item_ref[...], user_bf)
     mass = (counts + onehot) * jnp.exp(logits)
-    totals = jnp.sum(mass, 1, keepdims=True)
-    positive = jnp.sum(onehot * logits, 1, keepdims=True)
+    totals = jnp.sum(mass, 0, keepdims=True)
+    positive = jnp.sum(onehot * logits, 0, keepdims=True)
     rest = 1.0 - jnp.exp(positive) / totals
     row_loss = jnp.log(totals) - positive
     size = topk_ref[0]
@@ -271,20 +274,21 @@
     for bit in range(4):
         power = jnp.where((((size - 1) >> bit) & 1) == 1, power * square, power)
         square = square * square
-    ratio = as_column(ratios_ref[...])
+    ratio = ratios_ref[...]
     row_weight = ratio * (size.astype(F32) * power)
-    grad = (SHARP * row_weight) * (mass / totals - onehot)
-    pair_ref[:, :items] = grad.astype(BF)
-    pair_ref[:, items:] = user_bf
-    save_pair = pltpu.make_async_copy(pair_ref, pair_out, out_sems.at[5])
+    grad = mass * ((SHARP * row_weight) / totals) - onehot * (SHARP * row_weight)
+    pair_ref[:items, :] = grad.astype(BF)
+    save_pair = pltpu.make_async_copy(
+        pair_ref.at[:items, :], pair_out.at[:items, :], out_sems.at[5]
+    )
     save_pair.start()
-    numerator = jnp.sum(row_weight * row_loss, 0, keepdims=True)
+    numerator = jnp.sum(row_weight * row_loss, 1, keepdims=True)
     lanes = lax.broadcasted_iota(jnp.int32, sums_ref.shape[1:], 1)
-    both = jnp.where(lanes == 0, numerator, jnp.sum(ratio, 0, keepdims=True))
+    both = jnp.where(lanes == 0, numerator, jnp.sum(ratio, 1, keepdims=True))
     sums_ref[...] = jnp.broadcast_to(both[None], sums_ref.shape)
     save_sums = pltpu.make_async_copy(sums_ref, sums_out, out_sems.at[4])
     save_sums.start()
-    for copy in [save_user, save_item, save_pre, save_normed, save_sums, save_pair]:
+    for copy in [save_user, save_half, save_pre, save_normed, save_sums, save_pair]:
         copy.wait()
 
 
@@ -296,14 +300,13 @@
     return pl.pallas_call(
         forward_kernel,
         in_specs=vmem(3) + hbm(2) + vmem(3) + [pl.BlockSpec(memory_space=pltpu.SMEM)],
-        out_specs=vmem(2) + hbm(6),
+        out_specs=vmem(2) + hbm(5),
         out_shape=[
             jax.ShapeDtypeStruct((rows, 1), F32),
             jax.ShapeDtypeStruct((rows, 1), F32),
-            pltpu.HBM((rows, items + width), BF),
+            pltpu.HBM((items + width // 128 * rows, 128), BF),
             pltpu.HBM((copies, 8, 128), F32),
             pltpu.HBM((rows, width), F32),
-            pltpu.HBM((items, width), BF),
             pltpu.HBM((rows, 4 * width), BF),
             pltpu.HBM((rows, width), F32),
         ],
@@ -311,7 +314,7 @@
             pltpu.VMEM((rows, 4 * width), BF),
             pltpu.VMEM((rows, width), F32),
             pltpu.VMEM((rows, width), F32),
-            pltpu.VMEM((rows, items + width), BF),
+            pltpu.VMEM((items + width // 128 * rows, 128), BF),
             pltpu.VMEM((copies, 8, 128), F32),
             pltpu.VMEM((rows, width), F32),
             pltpu.VMEM((items, width), BF),
@@ -332,24 +335,30 @@
     load.start()
     chips, _, block, width = ditem_ref.shape
     items = chips * 2 * block
+    lane = own_ref.shape[1]
+    rows = (own_ref.shape[0] - items) * lane // width
     core = lax.axis_index("c")
     load.wait()
-    users = jnp.concatenate([own_ref[:, items:], other_ref[:, items:]], 0)
-    grads = jnp.concatenate([own_ref[:, :items], other_ref[:, :items]], 0)
+    users = []
+    for source in (own_ref, other_ref):
+        parts = [
+            source[items + n * rows : items + (n + 1) * rows, :] for n in range(width // lane)
+        ]
+        users.append(jnp.concatenate(parts, 1))
+    users = jnp.concatenate(users, 0)
+    grads = jnp.concatenate([own_ref[:items, :], other_ref[:items, :]], 1)
     steps = 4
     part = chips // steps
     for step in range(steps):
         at = slice(step * part, (step + 1) * part)
-        some = grads[:, step * items // steps : (step + 1) * items // steps]
-        ditem_ref[at] = dot_tn(some, users).astype(BF).reshape(part, 2, block, width)
+        some = grads[step * items // steps : (step + 1) * items // steps]
+        ditem_ref[at] = dot_nn(some, users).astype(BF).reshape(part, 2, block, width)
     back = pltpu.make_async_copy(ditem_ref.at[:, core], out_ref, out_sem)
     back.start()
     back.wait()
 
 
-def items_pass(own, other, chips, items):
-    rows, columns = own.shape
-    width = columns - items
+def items_pass(own, other, chips, items, width):
     block = items // (2 * chips)
     return pl.pallas_call(
         items_kernel,
@@ -357,13 +366,13 @@
         out_specs=vmem(1)[0],
         out_shape=jax.ShapeDtypeStruct((chips, block, width), BF),
         scratch_shapes=[
-            pltpu.VMEM((rows, columns), BF),
+            pltpu.VMEM(own.shape, BF),
             pltpu.VMEM((chips, 2, block, width), BF),
             pltpu.SemaphoreType.DMA,
             pltpu.SemaphoreType.DMA,
         ],
         compiler_params=pltpu.CompilerParams(**PARAMS),
-        cost_estimate=estimate(4 * rows * items * width, 4 * 1024 * 1024),
+        cost_estimate=estimate(512 * items * width, 4 * 1024 * 1024),
         name="items_pass",
     )(*in_hbm(own), other)
 
@@ -409,32 +418,33 @@
 
 
 def back_kernel(
-    invd_ref, segments_ref, invo_ref, pair_in, item_in, user_in, near_in, far_in, normed_in, pre_in,
+    invd_ref, segments_ref, invo_ref, pair_in, user_in, near_in, far_in, normed_in, pre_in,
     out_ref,
-    grad_ref, item_ref, user_ref, weight_ref, normed_ref, pre_ref, sems, weight_sems,
+    grad_ref, near_ref, far_ref, user_ref, weight_ref, normed_ref, pre_ref, sems, weight_sems,
 ):
     rows, width = normed_ref.shape
-    items = item_ref.shape[0]
+    items = grad_ref.shape[0]
     head = width // HEADS
     loads = [
-        (pair_in.at[:, :items], grad_ref), (item_in, item_ref), (user_in, user_ref),
-        (normed_in, normed_ref), (pre_in, pre_ref),
+        (pair_in.at[:items, :], grad_ref), (near_in.at[:, :, width:], near_ref),
+        (far_in.at[:, :, width:], far_ref), (user_in, user_ref), (normed_in, normed_ref),
+        (pre_in, pre_ref),
     ]
     loads = [pltpu.make_async_copy(p, q, sems.at[n]) for n, (p, q) in enumerate(loads)]
     into = weight_copies(near_in, far_in, weight_ref, weight_sems)
-    for copy in loads[:3] + into + loads[3:]:
+    for copy in loads[:4] + into + loads[4:]:
         copy.start()
     mask = causal_mask(segments_ref[...])
-    for copy in loads[:3]:
+    for copy in loads[:4]:
         copy.wait()
     user = user_ref[...]
-    d_user = dot_nn(grad_ref[...], item_ref[...])
+    d_user = dot_tn(grad_ref[...], unit_items(near_ref, far_ref, items))
     d_output = invo_ref[...] * (d_user - user * jnp.sum(user * d_user, 1, keepdims=True))
     for copy in into:
         copy.wait()
     d_gated = dot_nt(d_output.astype(BF), weight_ref[...].reshape(width, width))
-    loads[3].wait()
     loads[4].wait()
+    loads[5].wait()
     normed = normed_ref[...]
     gate = pre_ref[:, :width].astype(F32)
     gate_s = sigmoid(gate)
@@ -478,29 +488,30 @@
             out_ref[:, start : start + head] = grad * rate
 
 
-def back_pass(inv_dev, segments, inv_out, pair, item, user, near, far, normed, pre):
+def back_pass(inv_dev, segments, inv_out, pair, user, near, far, normed, pre):
     rows, width = normed.shape
-    items = item.shape[0]
     members, block = near.shape[:2]
+    items = members * block
     return pl.pallas_call(
         back_kernel,
-        in_specs=vmem(3) + hbm(7),
+        in_specs=vmem(3) + hbm(6),
         out_specs=vmem(1)[0],
         out_shape=jax.ShapeDtypeStruct((rows, 4 * width), F32),
         scratch_shapes=[
-            pltpu.VMEM((rows, items), BF),
-            pltpu.VMEM((items, width), BF),
+            pltpu.VMEM((items, rows), BF),
+            pltpu.VMEM((members, block, width // 2), BF),
+            pltpu.VMEM((members, block, width // 2), BF),
             pltpu.VMEM((rows, width), F32),
             pltpu.VMEM((members, 2, block, width), BF),
             pltpu.VMEM((rows, width), F32),
             pltpu.VMEM((rows, 4 * width), BF),
-            pltpu.SemaphoreType.DMA((5,)),
+            pltpu.SemaphoreType.DMA((6,)),
             pltpu.SemaphoreType.DMA((2 * PLANES,)),
         ],
         compiler_params=pltpu.CompilerParams(**PARAMS),
         cost_estimate=estimate(2 * rows * width * 2304, 8 * 1024 * 1024),
         name="back_pass",
-    )(inv_dev, segments, inv_out, *in_hbm(pair, item, user, near, far, normed, pre))
+    )(inv_dev, segments, inv_out, *in_hbm(pair, user, near, far, normed, pre))
 
 
 def finish_kernel(
@@ -580,17 +591,17 @@
             parts.append(lax.ppermute(mine_part, "z", pairs))
         near = jnp.concatenate(parts + [share[:, :, size:]], 2)
         far = lax.ppermute(near, "c", [(0, 1), (1, 0)])
-    inv_dev, inv_out, pair, sums, user, item, pre, normed = forward_pass(
+    inv_dev, inv_out, pair, sums, user, pre, normed = forward_pass(
         pack_rows, segments, got, near, far, negatives, targets, ratios, topk, 2 * groups
     )
     with jax.named_scope("sums"):
         sums = lax.all_to_all(sums, ("z", "c"), 0, 0, tiled=True)
     with jax.named_scope("items_back"):
         pair_other = lax.ppermute(pair, "c", [(0, 1), (1, 0)])
-        d_item = items_pass(pair, pair_other, members // 2, members * mine)
+        d_item = items_pass(pair, pair_other, members // 2, members * mine, width)
         d_item, inv_out = join(d_item, sums, inv_out)
         got_item = lax.all_to_all(d_item, ("x", "y"), 0, 0, tiled=True)
-    d_act = back_pass(inv_dev, segments, inv_out, pair, item, user, near, far, normed, pre)
+    d_act = back_pass(inv_dev, segments, inv_out, pair, user, near, far, normed, pre)
     loss, d_proj, d_table = finish(got_item, table, d_act)
     return (loss[0, :1], d_proj, d_table)
 

time: 117 us -> 117 us (level)
  no operation moved by 1% of the time
where the time goes in v3:
time: 117 us; the launch traced here: 115 us
  starting transfers between devices  52.5 us (45%)
  waiting for transfers between devices  38.1 us (33%)
  Pallas kernels  18.9 us (16%)
  local copies, waits for them, and re-layouts  4.08 us (3%)
  between operations  1.49 us (1%)
    ppermute x3, starting transfers between devices, shards(): parts.append(lax.ppermute(mine_part, 'z', pairs))  14.9 us
    all_to_all x1, starting transfers between devices, shards(): sums = lax.all_to_all(sums, ('z', 'c'), 0, 0, tiled=True)  14.3 us
    all_to_all x1, waiting for transfers between devices, shards(): lax.all_to_all(share.reshape(members, mine, share.shape[1]), MEMBERS, 0,...  11 us
    all_to_all x1, waiting for transfers between devices, shards(): sums = lax.all_to_all(sums, ('z', 'c'), 0, 0, tiled=True)  10.5 us
    all_to_all x1, starting transfers between devices, shards(): lax.all_to_all(share.reshape(members, mine, share.shape[1]), MEMBERS, 0,...  10.5 us
    ppermute x3, waiting for transfers between devices, shards(): parts.append(lax.ppermute(mine_part, 'z', pairs))  8.07 us
    pallas_call x1, Pallas kernels, back_pass(): pl.pallas_call(back_kernel, in_specs=vmem(3) + hbm(6), out_specs=vmem(1)[...  5.36 us
    pallas_call x1, Pallas kernels, forward_pass(): pl.pallas_call(forward_kernel, in_specs=vmem(3) + hbm(2) + vmem(3) + [pl....  4.4 us
  transfers between devices with their start and end apart: 9, of which 7 were waited for; matrix products, arithmetic and copies ran while one was open for 4% of the time, Pallas kernels for 9%

profile of v3, /device:TPU:1, one launch (start us, length us, event | category | flops | bytes accessed | tf_op | source)
XLA Modules:
  0.0 115.0 jit_solution(12062496116494979363)
XLA Ops:
  0.6 1.8 %shared_blocks.1 = bf16[512,768]{1,0:T(8,128)(2,1)} custom-call(bf16[16,1024]{1,0:T(8,128)(2,1)} %table_ref.1, bf16[32,1024]{1,0:T(8,128)(2,1)} %weight_in.1), custom_call_target="tpu_custom_call" | custom-call | flops 786432 | bytes 786432 | tf_op jit(solution)/shard_map/shared/shared_blocks/pallas_call | solution.py:127
  2.4 10.5 %all-to-all-start.1 = ((bf16[32,16,768]{2,1,0:T(8,128)(2,1)}), bf16[32,16,768]{2,1,0:T(8,128)(2,1)S(1)}, u32[]{:S(2)}, u32[]{:S(2)}) async-start(bf16[32,16,768]{2,1,0:T(8,128)(2,1)} %bitcast.7), calls=%async_computation.1 | async-start | bytes 1572864 | tf_op jit(solution)/shard_map/shared/all_to_all | solution.py:577
  12.9 3.3 %send_blocks.1 = bf16[256,5120]{1,0:T(8,128)(2,1)} custom-call(s32[1,256]{1,0:T(1,128)} %slots_in.1, bf16[128,4096]{1,0:T(8,128)(2,1)} %proj_in.1, bf16[128,1024]{1,0:T(8,128)(2,1)} %resid_in.1), custom_call_target="tpu_custom_call" | custom-call | flops 335544320 | bytes 3932160 | tf_op jit(solution)/shard_map/route/send_blocks/pallas_call | solution.py:78
  16.2 11.0 %all-to-all-done.1 = bf16[32,16,768]{2,1,0:T(8,128)(2,1)S(1)} async-done(((bf16[32,16,768]{2,1,0:T(8,128)(2,1)}), bf16[32,16,768]{2,1,0:T(8,128)(2,1)S(1)}, u32[]{:S(2)}, u32[]{:S(2)}) %all-to-all-start.1) | async-done | bytes 786464 | tf_op jit(solution)/shard_map/shared/all_to_all | solution.py:577
  27.2 3.8 %all-to-all-start = ((bf16[32,8,5120]{2,1,0:T(8,128)(2,1)}), bf16[32,8,5120]{2,1,0:T(8,128)(2,1)S(1)}, u32[]{:S(2)}, u32[]{:S(2)}) async-start(bf16[32,8,5120]{2,1,0:T(8,128)(2,1)} %bitcast.6), calls=%async_computation | async-start | bytes 5242880 | tf_op jit(solution)/shard_map/route/all_to_all | solution.py:582
  31.1 0.0 copy-start.1
  31.1 0.0 copy-start.2
  31.1 0.0 copy-start.3
  31.1 0.0 copy-start.4
  31.1 0.0 copy-start.5
  31.1 0.8 fusion
  31.9 9.1 %collective-permute-start = (bf16[32,16,256]{2,1,0:T(8,128)(2,1)S(1)}, bf16[32,16,256]{2,1,0:T(8,128)(2,1)S(1)}, u32[]{:S(2)}, u32[]{:S(2)}) collective-permute-start(bf16[32,16,256]{2,1,0:T(8,128)(2,1)S(1)} %get-tuple-element.27), channel_id=1, source_target_pairs={{0,480},{32,0},{64,32},{96,64},{128,96},{160,128},{192,160},{224,1... | collective-permute-start | bytes 786440 | tf_op jit(solution)/shard_map/planes/ppermute | solution.py:591
  41.1 1.9 %collective-permute-start.1 = (bf16[32,16,256]{2,1,0:T(8,128)(2,1)S(1)}, bf16[32,16,256]{2,1,0:T(8,128)(2,1)S(1)}, u32[]{:S(2)}, u32[]{:S(2)}) collective-permute-start(bf16[32,16,256]{2,1,0:T(8,128)(2,1)S(1)} %get-tuple-element.27), channel_id=1, source_target_pairs={{0,32},{32,64},{64,96},{96,128},{128,160},{160,192},{192,224},{224... | collective-permute-start | bytes 786440 | tf_op jit(solution)/shard_map/planes/ppermute | solution.py:591
  43.0 3.8 %collective-permute-start.2 = (bf16[32,16,256]{2,1,0:T(8,128)(2,1)S(1)}, bf16[32,16,256]{2,1,0:T(8,128)(2,1)S(1)}, u32[]{:S(2)}, u32[]{:S(2)}) collective-permute-start(bf16[32,16,256]{2,1,0:T(8,128)(2,1)S(1)} %get-tuple-element.27), channel_id=1, source_target_pairs={{0,448},{32,480},{64,0},{96,32},{128,64},{160,96},{192,128},{224,1... | collective-permute-start | bytes 786440 | tf_op jit(solution)/shard_map/planes/ppermute | solution.py:591
  46.8 0.0 collective-permute-done
  46.8 0.8 constant_dynamic-update-slice_fusion.2
  47.6 3.9 %collective-permute-done.1 = bf16[32,16,256]{2,1,0:T(8,128)(2,1)S(1)} collective-permute-done((bf16[32,16,256]{2,1,0:T(8,128)(2,1)S(1)}, bf16[32,16,256]{2,1,0:T(8,128)(2,1)S(1)}, u32[]{:S(2)}, u32[]{:S(2)}) %collective-permute-start.1) | collective-permute-done | bytes 262176 | tf_op jit(solution)/shard_map/planes/ppermute | solution.py:591
  51.5 0.8 constant_dynamic-update-slice_fusion.1
  52.3 4.1 %collective-permute-done.2 = bf16[32,16,256]{2,1,0:T(8,128)(2,1)S(1)} collective-permute-done((bf16[32,16,256]{2,1,0:T(8,128)(2,1)S(1)}, bf16[32,16,256]{2,1,0:T(8,128)(2,1)S(1)}, u32[]{:S(2)}, u32[]{:S(2)}) %collective-permute-start.2) | collective-permute-done | bytes 262176 | tf_op jit(solution)/shard_map/planes/ppermute | solution.py:591
  56.4 0.8 constant_dynamic-update-slice_fusion
  57.2 0.9 slice_dynamic-update-slice_fusion.near_in
  58.1 3.2 %collective-permute-start.3 = (bf16[32,16,1536]{2,1,0:T(8,128)(2,1)}, bf16[32,16,1536]{2,1,0:T(8,128)(2,1)}, u32[]{:S(2)}, u32[]{:S(2)}) collective-permute-start(bf16[32,16,1536]{2,1,0:T(8,128)(2,1)} %slice_dynamic-update-slice_fusion.near_in), channel_id=1, source_target_pairs={{0,1},{1,0},{2,3},{3,2},{4,5},{5,4},{6,7},{7,6},{8,9},{9,8},{10,11... | collective-permute-start | bytes 4718600 | tf_op jit(solution)/shard_map/planes/ppermute | solution.py:593
  62.0 2.9 %all-to-all-done = bf16[32,8,5120]{2,1,0:T(8,128)(2,1)S(1)} async-done(((bf16[32,8,5120]{2,1,0:T(8,128)(2,1)}), bf16[32,8,5120]{2,1,0:T(8,128)(2,1)S(1)}, u32[]{:S(2)}, u32[]{:S(2)}) %all-to-all-start) | async-done | bytes 2621472 | tf_op jit(solution)/shard_map/route/all_to_all | solution.py:582
  64.9 0.0 collective-permute-done.3.far_in
  64.9 0.0 copy-done.1
  64.9 0.0 copy-done.2
  64.9 0.0 copy-done.3
  64.9 0.0 copy-done.4
  64.9 0.0 copy-done.5
  64.9 4.4 %forward_pass.1 = (f32[128,1]{1,0:T(8,128)S(1)}, f32[128,1]{1,0:T(8,128)S(1)}, bf16[1536,128]{1,0:T(8,128)(2,1)}, f32[32,8,128]{2,1,0:T(8,128)}, f32[128,1024]{1...) custom-call(s32[1,128]{1,0:T(1,128)S(1)} %copy-done.3, s32[1,128]{1,0:T(1,128)S(1)} %copy-done.1, ...), custom_call_target="tpu_custom_call" | custom-call | flops 738197504 | bytes 12582912 | tf_op jit(solution)/shard_map/forward_pass/pallas_call | solution.py:300
  69.3 14.3 %all-to-all-start.2 = ((f32[32,8,128]{2,1,0:T(8,128)}), f32[32,8,128]{2,1,0:T(8,128)S(1)}, u32[]{:S(2)}, u32[]{:S(2)}) async-start(f32[32,8,128]{2,1,0:T(8,128)} %get-tuple-element.16), calls=%async_computation.2 | async-start | bytes 262144 | tf_op jit(solution)/shard_map/sums/all_to_all | solution.py:598
  83.7 2.1 %collective-permute-start.4 = (bf16[1536,128]{1,0:T(8,128)(2,1)}, bf16[1536,128]{1,0:T(8,128)(2,1)S(1)}, u32[]{:S(2)}, u32[]{:S(2)}) collective-permute-start(bf16[1536,128]{1,0:T(8,128)(2,1)} %get-tuple-element.15.own_in.pair_in), channel_id=1, source_target_pairs={{0,1},{1,0},{2,3},{3,2},{4,5},{5,4},{6,7},{7,6},{8,9},{9,8},{10,11... | collective-permute-start | bytes 1179656 | tf_op jit(solution)/shard_map/items_back/ppermute | solution.py:600
  85.8 1.7 %collective-permute-done.4.other_ref = bf16[1536,128]{1,0:T(8,128)(2,1)S(1)} collective-permute-done((bf16[1536,128]{1,0:T(8,128)(2,1)}, bf16[1536,128]{1,0:T(8,128)(2,1)S(1)}, u32[]{:S(2)}, u32[]{:S(2)}) %collective-permute-start.4) | collective-permute-done | bytes 393248 | tf_op jit(solution)/shard_map/items_back/ppermute | solution.py:600
  87.5 1.5 %items_pass.1.ditem_ref = bf16[16,16,1024]{2,1,0:T(8,128)(2,1)S(1)} custom-call(bf16[1536,128]{1,0:T(8,128)(2,1)} %get-tuple-element.15.own_in.pair_in, bf16[1536,128]{1,0:T(8,128)(2,1)S(1)} %collective-permute-done.4.other_ref), custom_call_target="tpu_custom_call" | custom-call | flops 268435456 | bytes 4194304 | tf_op jit(solution)/shard_map/items_back/items_pass/pallas_call | solution.py:363
  89.0 10.5 %all-to-all-done.2.sums_ref = f32[32,8,128]{2,1,0:T(8,128)S(1)} async-done(((f32[32,8,128]{2,1,0:T(8,128)}), f32[32,8,128]{2,1,0:T(8,128)S(1)}, u32[]{:S(2)}, u32[]{:S(2)}) %all-to-all-start.2) | async-done | bytes 131104 | tf_op jit(solution)/shard_map/sums/all_to_all | solution.py:598
  99.5 0.9 join.1
  100.4 3.6 %all-to-all-start.3 = ((bf16[16,16,1152]{2,1,0:T(8,128)(2,1)}), bf16[16,16,1152]{2,1,0:T(8,128)(2,1)S(1)}, u32[]{:S(2)}, u32[]{:S(2)}) async-start(bf16[16,16,1152]{2,1,0:T(8,128)(2,1)} %get-tuple-element.18), calls=%async_computation.3 | async-start | bytes 1179648 | tf_op jit(solution)/shard_map/items_back/all_to_all | solution.py:603
  104.0 0.0 copy-start
  104.0 5.4 %back_pass.1.act_ref = f32[128,4096]{1,0:T(8,128)S(1)} custom-call(f32[128,1]{1,0:T(8,128)S(1)} %get-tuple-element.19.invd_ref, s32[1,128]{1,0:T(1,128)S(1)} %copy-done.1, f32[128,1]{1,0:T(8,128)S(1)} %get-tuple-element.20.invo_ref, bf16[1536,128]{1,0:T(8,128)(2,1)} %get-tuple-element.15.own_in.pair_in, f32[128,1024]{1,0:T(8,128)} %get-tuple-element.21.user_in, ...), custom_call_target="tpu_custom_call" | custom-call | flops 603979776 | bytes 8388608 | tf_op jit(solution)/shard_map/back_pass/pallas_call | solution.py:495
  109.4 3.9 %all-to-all-done.3.got_ref = bf16[16,16,1152]{2,1,0:T(8,128)(2,1)S(1)} async-done(((bf16[16,16,1152]{2,1,0:T(8,128)(2,1)}), bf16[16,16,1152]{2,1,0:T(8,128)(2,1)S(1)}, u32[]{:S(2)}, u32[]{:S(2)}) %all-to-all-start.3) | async-done | bytes 589856 | tf_op jit(solution)/shard_map/items_back/all_to_all | solution.py:603
  113.3 0.0 copy-done
  113.3 1.7 %finish.1 = (f32[1,128]{1,0:T(1,128)}, bf16[128,4096]{1,0:T(8,128)(2,1)}, f32[16,1024]{1,0:T(8,128)}) custom-call(bf16[16,16,1152]{2,1,0:T(8,128)(2,1)S(1)} %all-to-all-done.3.got_ref, bf16[16,1024]{1,0:T(8,128)(2,1)S(1)} %copy-done, f32[128,4096]{1,0:T(8,128)S(1)} %back_pass.1.act_ref), custom_call_target="tpu_custom_call" | custom-call | flops 524288 | bytes 3145728 | tf_op jit(solution)/shard_map/finish/pallas_call | solution.py:549
Async XLA Ops:
  2.4 24.8 %all-to-all-start.1 = ((bf16[32,16,768]{2,1,0:T(8,128)(2,1)}), bf16[32,16,768]{2,1,0:T(8,128)(2,1)S(1)}, u32[]{:S(2)}, u32[]{:S(2)}) async-start(bf16[32,16,768]{2,1,0:T(8,128)(2,1)} %bitcast.7), calls=%async_computation.1 | async-start | bytes 1572864 | tf_op jit(solution)/shard_map/shared/all_to_all | solution.py:577
  27.2 37.7 %all-to-all-start = ((bf16[32,8,5120]{2,1,0:T(8,128)(2,1)}), bf16[32,8,5120]{2,1,0:T(8,128)(2,1)S(1)}, u32[]{:S(2)}, u32[]{:S(2)}) async-start(bf16[32,8,5120]{2,1,0:T(8,128)(2,1)} %bitcast.6), calls=%async_computation | async-start | bytes 5242880 | tf_op jit(solution)/shard_map/route/all_to_all | solution.py:582
  31.1 33.8 %copy-start.1 = (s32[1,128]{1,0:T(1,128)S(1)}, s32[1,128]{1,0:T(1,128)}, u32[]{:S(2)}) copy-start(s32[1,128]{1,0:T(1,128)} %segments_ref.3) | copy-start | bytes 1540
  31.1 33.8 %copy-start.2 = (s32[1,256]{1,0:T(1,128)S(1)}, s32[1,256]{1,0:T(1,128)}, u32[]{:S(2)}) copy-start(s32[1,256]{1,0:T(1,128)} %negatives_ref.1) | copy-start | bytes 3076
  31.1 33.8 %copy-start.3 = (s32[1,128]{1,0:T(1,128)S(1)}, s32[1,128]{1,0:T(1,128)}, u32[]{:S(2)}) copy-start(s32[1,128]{1,0:T(1,128)} %order_ref.1) | copy-start | bytes 1540
  31.1 33.8 %copy-start.4 = (s32[1,128]{1,0:T(1,128)S(1)}, s32[1,128]{1,0:T(1,128)}, u32[]{:S(2)}) copy-start(s32[1,128]{1,0:T(1,128)} %targets_ref.1) | copy-start | bytes 1540
  31.1 33.8 %copy-start.5 = (f32[1,128]{1,0:T(1,128)S(1)}, f32[1,128]{1,0:T(1,128)}, u32[]{:S(2)}) copy-start(f32[1,128]{1,0:T(1,128)} %ratios_ref.1) | copy-start | bytes 1540
  31.9 14.9 %collective-permute-start = (bf16[32,16,256]{2,1,0:T(8,128)(2,1)S(1)}, bf16[32,16,256]{2,1,0:T(8,128)(2,1)S(1)}, u32[]{:S(2)}, u32[]{:S(2)}) collective-permute-start(bf16[32,16,256]{2,1,0:T(8,128)(2,1)S(1)} %get-tuple-element.27), channel_id=1, source_target_pairs={{0,480},{32,0},{64,32},{96,64},{128,96},{160,128},{192,160},{224,1... | collective-permute-start | bytes 786440 | tf_op jit(solution)/shard_map/planes/ppermute | solution.py:591
  41.1 10.5 %collective-permute-start.1 = (bf16[32,16,256]{2,1,0:T(8,128)(2,1)S(1)}, bf16[32,16,256]{2,1,0:T(8,128)(2,1)S(1)}, u32[]{:S(2)}, u32[]{:S(2)}) collective-permute-start(bf16[32,16,256]{2,1,0:T(8,128)(2,1)S(1)} %get-tuple-element.27), channel_id=1, source_target_pairs={{0,32},{32,64},{64,96},{96,128},{128,160},{160,192},{192,224},{224... | collective-permute-start | bytes 786440 | tf_op jit(solution)/shard_map/planes/ppermute | solution.py:591
  43.0 13.4 %collective-permute-start.2 = (bf16[32,16,256]{2,1,0:T(8,128)(2,1)S(1)}, bf16[32,16,256]{2,1,0:T(8,128)(2,1)S(1)}, u32[]{:S(2)}, u32[]{:S(2)}) collective-permute-start(bf16[32,16,256]{2,1,0:T(8,128)(2,1)S(1)} %get-tuple-element.27), channel_id=1, source_target_pairs={{0,448},{32,480},{64,0},{96,32},{128,64},{160,96},{192,128},{224,1... | collective-permute-start | bytes 786440 | tf_op jit(solution)/shard_map/planes/ppermute | solution.py:591
  58.1 6.8 %collective-permute-start.3 = (bf16[32,16,1536]{2,1,0:T(8,128)(2,1)}, bf16[32,16,1536]{2,1,0:T(8,128)(2,1)}, u32[]{:S(2)}, u32[]{:S(2)}) collective-permute-start(bf16[32,16,1536]{2,1,0:T(8,128)(2,1)} %slice_dynamic-update-slice_fusion.near_in), channel_id=1, source_target_pairs={{0,1},{1,0},{2,3},{3,2},{4,5},{5,4},{6,7},{7,6},{8,9},{9,8},{10,11... | collective-permute-start | bytes 4718600 | tf_op jit(solution)/shard_map/planes/ppermute | solution.py:593
  69.3 30.2 %all-to-all-start.2 = ((f32[32,8,128]{2,1,0:T(8,128)}), f32[32,8,128]{2,1,0:T(8,128)S(1)}, u32[]{:S(2)}, u32[]{:S(2)}) async-start(f32[32,8,128]{2,1,0:T(8,128)} %get-tuple-element.16), calls=%async_computation.2 | async-start | bytes 262144 | tf_op jit(solution)/shard_map/sums/all_to_all | solution.py:598
  83.7 3.8 %collective-permute-start.4 = (bf16[1536,128]{1,0:T(8,128)(2,1)}, bf16[1536,128]{1,0:T(8,128)(2,1)S(1)}, u32[]{:S(2)}, u32[]{:S(2)}) collective-permute-start(bf16[1536,128]{1,0:T(8,128)(2,1)} %get-tuple-element.15.own_in.pair_in), channel_id=1, source_target_pairs={{0,1},{1,0},{2,3},{3,2},{4,5},{5,4},{6,7},{7,6},{8,9},{9,8},{10,11... | collective-permute-start | bytes 1179656 | tf_op jit(solution)/shard_map/items_back/ppermute | solution.py:600
  100.4 12.9 %all-to-all-start.3 = ((bf16[16,16,1152]{2,1,0:T(8,128)(2,1)}), bf16[16,16,1152]{2,1,0:T(8,128)(2,1)S(1)}, u32[]{:S(2)}, u32[]{:S(2)}) async-start(bf16[16,16,1152]{2,1,0:T(8,128)(2,1)} %get-tuple-element.18), calls=%async_computation.3 | async-start | bytes 1179648 | tf_op jit(solution)/shard_map/items_back/all_to_all | solution.py:603
  104.0 9.3 %copy-start = (bf16[16,1024]{1,0:T(8,128)(2,1)S(1)}, bf16[16,1024]{1,0:T(8,128)(2,1)}, u32[]{:S(2)}) copy-start(bf16[16,1024]{1,0:T(8,128)(2,1)} %table_ref.1) | copy-start | bytes 98308

commit v4 on v3

--- a/solution.py
+++ b/solution.py
@@ -29,7 +29,7 @@
 
 
 def sigmoid(values):
-    return 1.0 / (1.0 + jnp.exp(-values))
+    return 0.5 + 0.5 * jnp.tanh(0.5 * values)
 
 
 def vmem(count):
@@ -558,7 +558,7 @@
         scratch_shapes=[
             pltpu.VMEM((rows, columns), BF),
             pltpu.VMEM(table.shape, F32),
-            pltpu.SemaphoreType.DMA((5,)),
+            pltpu.SemaphoreType.DMA((9,)),
         ],
         compiler_params=pltpu.CompilerParams(**PARAMS),
         cost_estimate=estimate(rows * columns, rows * columns * 6),

time: 117 us -> 117 us (level)
  no operation moved by 1% of the time
where the time goes in v4:
time: 117 us; the launch traced here: 115 us
  starting transfers between devices  52.5 us (45%)
  waiting for transfers between devices  38.1 us (33%)
  Pallas kernels  18.9 us (16%)
  local copies, waits for them, and re-layouts  4.08 us (3%)
  between operations  1.49 us (1%)
    ppermute x3, starting transfers between devices, shards(): parts.append(lax.ppermute(mine_part, 'z', pairs))  14.9 us
    all_to_all x1, starting transfers between devices, shards(): sums = lax.all_to_all(sums, ('z', 'c'), 0, 0, tiled=True)  14.3 us
    all_to_all x1, waiting for transfers between devices, shards(): lax.all_to_all(share.reshape(members, mine, share.shape[1]), MEMBERS, 0,...  11 us
    all_to_all x1, waiting for transfers between devices, shards(): sums = lax.all_to_all(sums, ('z', 'c'), 0, 0, tiled=True)  10.5 us
    all_to_all x1, starting transfers between devices, shards(): lax.all_to_all(share.reshape(members, mine, share.shape[1]), MEMBERS, 0,...  10.5 us
    ppermute x3, waiting for transfers between devices, shards(): parts.append(lax.ppermute(mine_part, 'z', pairs))  8.07 us
    pallas_call x1, Pallas kernels, back_pass(): pl.pallas_call(back_kernel, in_specs=vmem(3) + hbm(6), out_specs=vmem(1)[...  5.34 us
    pallas_call x1, Pallas kernels, forward_pass(): pl.pallas_call(forward_kernel, in_specs=vmem(3) + hbm(2) + vmem(3) + [pl....  4.4 us
  transfers between devices with their start and end apart: 9, of which 7 were waited for; matrix products, arithmetic and copies ran while one was open for 4% of the time, Pallas kernels for 9%

profile of v4, /device:TPU:1, one launch (start us, length us, event | category | flops | bytes accessed | tf_op | source)
XLA Modules:
  0.0 115.0 jit_solution(5987695810451450457)
XLA Ops:
  0.6 1.8 %shared_blocks.1 = bf16[512,768]{1,0:T(8,128)(2,1)} custom-call(bf16[16,1024]{1,0:T(8,128)(2,1)} %table_ref.1, bf16[32,1024]{1,0:T(8,128)(2,1)} %weight_in.1), custom_call_target="tpu_custom_call" | custom-call | flops 786432 | bytes 786432 | tf_op jit(solution)/shard_map/shared/shared_blocks/pallas_call | solution.py:127
  2.4 10.5 %all-to-all-start.1 = ((bf16[32,16,768]{2,1,0:T(8,128)(2,1)}), bf16[32,16,768]{2,1,0:T(8,128)(2,1)S(1)}, u32[]{:S(2)}, u32[]{:S(2)}) async-start(bf16[32,16,768]{2,1,0:T(8,128)(2,1)} %bitcast.7), calls=%async_computation.1 | async-start | bytes 1572864 | tf_op jit(solution)/shard_map/shared/all_to_all | solution.py:577
  12.9 3.3 %send_blocks.1 = bf16[256,5120]{1,0:T(8,128)(2,1)} custom-call(s32[1,256]{1,0:T(1,128)} %slots_in.1, bf16[128,4096]{1,0:T(8,128)(2,1)} %proj_in.1, bf16[128,1024]{1,0:T(8,128)(2,1)} %resid_in.1), custom_call_target="tpu_custom_call" | custom-call | flops 335544320 | bytes 3932160 | tf_op jit(solution)/shard_map/route/send_blocks/pallas_call | solution.py:78
  16.2 11.0 %all-to-all-done.1 = bf16[32,16,768]{2,1,0:T(8,128)(2,1)S(1)} async-done(((bf16[32,16,768]{2,1,0:T(8,128)(2,1)}), bf16[32,16,768]{2,1,0:T(8,128)(2,1)S(1)}, u32[]{:S(2)}, u32[]{:S(2)}) %all-to-all-start.1) | async-done | bytes 786464 | tf_op jit(solution)/shard_map/shared/all_to_all | solution.py:577
  27.2 3.8 %all-to-all-start = ((bf16[32,8,5120]{2,1,0:T(8,128)(2,1)}), bf16[32,8,5120]{2,1,0:T(8,128)(2,1)S(1)}, u32[]{:S(2)}, u32[]{:S(2)}) async-start(bf16[32,8,5120]{2,1,0:T(8,128)(2,1)} %bitcast.6), calls=%async_computation | async-start | bytes 5242880 | tf_op jit(solution)/shard_map/route/all_to_all | solution.py:582
  31.1 0.0 copy-start.1
  31.1 0.0 copy-start.2
  31.1 0.0 copy-start.3
  31.1 0.0 copy-start.4
  31.1 0.0 copy-start.5
  31.1 0.8 fusion
  31.9 9.1 %collective-permute-start = (bf16[32,16,256]{2,1,0:T(8,128)(2,1)S(1)}, bf16[32,16,256]{2,1,0:T(8,128)(2,1)S(1)}, u32[]{:S(2)}, u32[]{:S(2)}) collective-permute-start(bf16[32,16,256]{2,1,0:T(8,128)(2,1)S(1)} %get-tuple-element.27), channel_id=1, source_target_pairs={{0,480},{32,0},{64,32},{96,64},{128,96},{160,128},{192,160},{224,1... | collective-permute-start | bytes 786440 | tf_op jit(solution)/shard_map/planes/ppermute | solution.py:591
  41.1 1.9 %collective-permute-start.1 = (bf16[32,16,256]{2,1,0:T(8,128)(2,1)S(1)}, bf16[32,16,256]{2,1,0:T(8,128)(2,1)S(1)}, u32[]{:S(2)}, u32[]{:S(2)}) collective-permute-start(bf16[32,16,256]{2,1,0:T(8,128)(2,1)S(1)} %get-tuple-element.27), channel_id=1, source_target_pairs={{0,32},{32,64},{64,96},{96,128},{128,160},{160,192},{192,224},{224... | collective-permute-start | bytes 786440 | tf_op jit(solution)/shard_map/planes/ppermute | solution.py:591
  43.0 3.8 %collective-permute-start.2 = (bf16[32,16,256]{2,1,0:T(8,128)(2,1)S(1)}, bf16[32,16,256]{2,1,0:T(8,128)(2,1)S(1)}, u32[]{:S(2)}, u32[]{:S(2)}) collective-permute-start(bf16[32,16,256]{2,1,0:T(8,128)(2,1)S(1)} %get-tuple-element.27), channel_id=1, source_target_pairs={{0,448},{32,480},{64,0},{96,32},{128,64},{160,96},{192,128},{224,1... | collective-permute-start | bytes 786440 | tf_op jit(solution)/shard_map/planes/ppermute | solution.py:591
  46.8 0.0 collective-permute-done
  46.8 0.8 constant_dynamic-update-slice_fusion.2
  47.6 3.9 %collective-permute-done.1 = bf16[32,16,256]{2,1,0:T(8,128)(2,1)S(1)} collective-permute-done((bf16[32,16,256]{2,1,0:T(8,128)(2,1)S(1)}, bf16[32,16,256]{2,1,0:T(8,128)(2,1)S(1)}, u32[]{:S(2)}, u32[]{:S(2)}) %collective-permute-start.1) | collective-permute-done | bytes 262176 | tf_op jit(solution)/shard_map/planes/ppermute | solution.py:591
  51.5 0.8 constant_dynamic-update-slice_fusion.1
  52.3 4.1 %collective-permute-done.2 = bf16[32,16,256]{2,1,0:T(8,128)(2,1)S(1)} collective-permute-done((bf16[32,16,256]{2,1,0:T(8,128)(2,1)S(1)}, bf16[32,16,256]{2,1,0:T(8,128)(2,1)S(1)}, u32[]{:S(2)}, u32[]{:S(2)}) %collective-permute-start.2) | collective-permute-done | bytes 262176 | tf_op jit(solution)/shard_map/planes/ppermute | solution.py:591
  56.4 0.8 constant_dynamic-update-slice_fusion
  57.2 0.9 slice_dynamic-update-slice_fusion.near_in
  58.1 3.2 %collective-permute-start.3 = (bf16[32,16,1536]{2,1,0:T(8,128)(2,1)}, bf16[32,16,1536]{2,1,0:T(8,128)(2,1)}, u32[]{:S(2)}, u32[]{:S(2)}) collective-permute-start(bf16[32,16,1536]{2,1,0:T(8,128)(2,1)} %slice_dynamic-update-slice_fusion.near_in), channel_id=1, source_target_pairs={{0,1},{1,0},{2,3},{3,2},{4,5},{5,4},{6,7},{7,6},{8,9},{9,8},{10,11... | collective-permute-start | bytes 4718600 | tf_op jit(solution)/shard_map/planes/ppermute | solution.py:593
  62.0 2.9 %all-to-all-done = bf16[32,8,5120]{2,1,0:T(8,128)(2,1)S(1)} async-done(((bf16[32,8,5120]{2,1,0:T(8,128)(2,1)}), bf16[32,8,5120]{2,1,0:T(8,128)(2,1)S(1)}, u32[]{:S(2)}, u32[]{:S(2)}) %all-to-all-start) | async-done | bytes 2621472 | tf_op jit(solution)/shard_map/route/all_to_all | solution.py:582
  64.9 0.0 collective-permute-done.3.far_in
  64.9 0.0 copy-done.1
  64.9 0.0 copy-done.2
  64.9 0.0 copy-done.3
  64.9 0.0 copy-done.4
  64.9 0.0 copy-done.5
  64.9 4.4 %forward_pass.1 = (f32[128,1]{1,0:T(8,128)S(1)}, f32[128,1]{1,0:T(8,128)S(1)}, bf16[1536,128]{1,0:T(8,128)(2,1)}, f32[32,8,128]{2,1,0:T(8,128)}, f32[128,1024]{1...) custom-call(s32[1,128]{1,0:T(1,128)S(1)} %copy-done.3, s32[1,128]{1,0:T(1,128)S(1)} %copy-done.1, ...), custom_call_target="tpu_custom_call" | custom-call | flops 738197504 | bytes 12582912 | tf_op jit(solution)/shard_map/forward_pass/pallas_call | solution.py:300
  69.3 14.3 %all-to-all-start.2 = ((f32[32,8,128]{2,1,0:T(8,128)}), f32[32,8,128]{2,1,0:T(8,128)S(1)}, u32[]{:S(2)}, u32[]{:S(2)}) async-start(f32[32,8,128]{2,1,0:T(8,128)} %get-tuple-element.16), calls=%async_computation.2 | async-start | bytes 262144 | tf_op jit(solution)/shard_map/sums/all_to_all | solution.py:598
  83.7 2.1 %collective-permute-start.4 = (bf16[1536,128]{1,0:T(8,128)(2,1)}, bf16[1536,128]{1,0:T(8,128)(2,1)S(1)}, u32[]{:S(2)}, u32[]{:S(2)}) collective-permute-start(bf16[1536,128]{1,0:T(8,128)(2,1)} %get-tuple-element.15.own_in.pair_in), channel_id=1, source_target_pairs={{0,1},{1,0},{2,3},{3,2},{4,5},{5,4},{6,7},{7,6},{8,9},{9,8},{10,11... | collective-permute-start | bytes 1179656 | tf_op jit(solution)/shard_map/items_back/ppermute | solution.py:600
  85.8 1.7 %collective-permute-done.4.other_ref = bf16[1536,128]{1,0:T(8,128)(2,1)S(1)} collective-permute-done((bf16[1536,128]{1,0:T(8,128)(2,1)}, bf16[1536,128]{1,0:T(8,128)(2,1)S(1)}, u32[]{:S(2)}, u32[]{:S(2)}) %collective-permute-start.4) | collective-permute-done | bytes 393248 | tf_op jit(solution)/shard_map/items_back/ppermute | solution.py:600
  87.5 1.5 %items_pass.1.ditem_ref = bf16[16,16,1024]{2,1,0:T(8,128)(2,1)S(1)} custom-call(bf16[1536,128]{1,0:T(8,128)(2,1)} %get-tuple-element.15.own_in.pair_in, bf16[1536,128]{1,0:T(8,128)(2,1)S(1)} %collective-permute-done.4.other_ref), custom_call_target="tpu_custom_call" | custom-call | flops 268435456 | bytes 4194304 | tf_op jit(solution)/shard_map/items_back/items_pass/pallas_call | solution.py:363
  89.0 10.5 %all-to-all-done.2.sums_ref = f32[32,8,128]{2,1,0:T(8,128)S(1)} async-done(((f32[32,8,128]{2,1,0:T(8,128)}), f32[32,8,128]{2,1,0:T(8,128)S(1)}, u32[]{:S(2)}, u32[]{:S(2)}) %all-to-all-start.2) | async-done | bytes 131104 | tf_op jit(solution)/shard_map/sums/all_to_all | solution.py:598
  99.5 0.9 join.1
  100.4 3.6 %all-to-all-start.3 = ((bf16[16,16,1152]{2,1,0:T(8,128)(2,1)}), bf16[16,16,1152]{2,1,0:T(8,128)(2,1)S(1)}, u32[]{:S(2)}, u32[]{:S(2)}) async-start(bf16[16,16,1152]{2,1,0:T(8,128)(2,1)} %get-tuple-element.18), calls=%async_computation.3 | async-start | bytes 1179648 | tf_op jit(solution)/shard_map/items_back/all_to_all | solution.py:603
  104.0 0.0 copy-start
  104.0 5.3 %back_pass.1.act_ref = f32[128,4096]{1,0:T(8,128)S(1)} custom-call(f32[128,1]{1,0:T(8,128)S(1)} %get-tuple-element.19.invd_ref, s32[1,128]{1,0:T(1,128)S(1)} %copy-done.1, f32[128,1]{1,0:T(8,128)S(1)} %get-tuple-element.20.invo_ref, bf16[1536,128]{1,0:T(8,128)(2,1)} %get-tuple-element.15.own_in.pair_in, f32[128,1024]{1,0:T(8,128)} %get-tuple-element.21.user_in, ...), custom_call_target="tpu_custom_call" | custom-call | flops 603979776 | bytes 8388608 | tf_op jit(solution)/shard_map/back_pass/pallas_call | solution.py:495
  109.3 3.9 %all-to-all-done.3.got_ref = bf16[16,16,1152]{2,1,0:T(8,128)(2,1)S(1)} async-done(((bf16[16,16,1152]{2,1,0:T(8,128)(2,1)}), bf16[16,16,1152]{2,1,0:T(8,128)(2,1)S(1)}, u32[]{:S(2)}, u32[]{:S(2)}) %all-to-all-start.3) | async-done | bytes 589856 | tf_op jit(solution)/shard_map/items_back/all_to_all | solution.py:603
  113.3 0.0 copy-done
  113.3 1.7 %finish.1 = (f32[1,128]{1,0:T(1,128)}, bf16[128,4096]{1,0:T(8,128)(2,1)}, f32[16,1024]{1,0:T(8,128)}) custom-call(bf16[16,16,1152]{2,1,0:T(8,128)(2,1)S(1)} %all-to-all-done.3.got_ref, bf16[16,1024]{1,0:T(8,128)(2,1)S(1)} %copy-done, f32[128,4096]{1,0:T(8,128)S(1)} %back_pass.1.act_ref), custom_call_target="tpu_custom_call" | custom-call | flops 524288 | bytes 3145728 | tf_op jit(solution)/shard_map/finish/pallas_call | solution.py:549
Async XLA Ops:
  2.4 24.8 %all-to-all-start.1 = ((bf16[32,16,768]{2,1,0:T(8,128)(2,1)}), bf16[32,16,768]{2,1,0:T(8,128)(2,1)S(1)}, u32[]{:S(2)}, u32[]{:S(2)}) async-start(bf16[32,16,768]{2,1,0:T(8,128)(2,1)} %bitcast.7), calls=%async_computation.1 | async-start | bytes 1572864 | tf_op jit(solution)/shard_map/shared/all_to_all | solution.py:577
  27.2 37.7 %all-to-all-start = ((bf16[32,8,5120]{2,1,0:T(8,128)(2,1)}), bf16[32,8,5120]{2,1,0:T(8,128)(2,1)S(1)}, u32[]{:S(2)}, u32[]{:S(2)}) async-start(bf16[32,8,5120]{2,1,0:T(8,128)(2,1)} %bitcast.6), calls=%async_computation | async-start | bytes 5242880 | tf_op jit(solution)/shard_map/route/all_to_all | solution.py:582
  31.1 33.8 %copy-start.1 = (s32[1,128]{1,0:T(1,128)S(1)}, s32[1,128]{1,0:T(1,128)}, u32[]{:S(2)}) copy-start(s32[1,128]{1,0:T(1,128)} %segments_ref.3) | copy-start | bytes 1540
  31.1 33.8 %copy-start.2 = (s32[1,256]{1,0:T(1,128)S(1)}, s32[1,256]{1,0:T(1,128)}, u32[]{:S(2)}) copy-start(s32[1,256]{1,0:T(1,128)} %negatives_ref.1) | copy-start | bytes 3076
  31.1 33.8 %copy-start.3 = (s32[1,128]{1,0:T(1,128)S(1)}, s32[1,128]{1,0:T(1,128)}, u32[]{:S(2)}) copy-start(s32[1,128]{1,0:T(1,128)} %order_ref.1) | copy-start | bytes 1540
  31.1 33.8 %copy-start.4 = (s32[1,128]{1,0:T(1,128)S(1)}, s32[1,128]{1,0:T(1,128)}, u32[]{:S(2)}) copy-start(s32[1,128]{1,0:T(1,128)} %targets_ref.1) | copy-start | bytes 1540
  31.1 33.8 %copy-start.5 = (f32[1,128]{1,0:T(1,128)S(1)}, f32[1,128]{1,0:T(1,128)}, u32[]{:S(2)}) copy-start(f32[1,128]{1,0:T(1,128)} %ratios_ref.1) | copy-start | bytes 1540
  31.9 14.9 %collective-permute-start = (bf16[32,16,256]{2,1,0:T(8,128)(2,1)S(1)}, bf16[32,16,256]{2,1,0:T(8,128)(2,1)S(1)}, u32[]{:S(2)}, u32[]{:S(2)}) collective-permute-start(bf16[32,16,256]{2,1,0:T(8,128)(2,1)S(1)} %get-tuple-element.27), channel_id=1, source_target_pairs={{0,480},{32,0},{64,32},{96,64},{128,96},{160,128},{192,160},{224,1... | collective-permute-start | bytes 786440 | tf_op jit(solution)/shard_map/planes/ppermute | solution.py:591
  41.1 10.5 %collective-permute-start.1 = (bf16[32,16,256]{2,1,0:T(8,128)(2,1)S(1)}, bf16[32,16,256]{2,1,0:T(8,128)(2,1)S(1)}, u32[]{:S(2)}, u32[]{:S(2)}) collective-permute-start(bf16[32,16,256]{2,1,0:T(8,128)(2,1)S(1)} %get-tuple-element.27), channel_id=1, source_target_pairs={{0,32},{32,64},{64,96},{96,128},{128,160},{160,192},{192,224},{224... | collective-permute-start | bytes 786440 | tf_op jit(solution)/shard_map/planes/ppermute | solution.py:591
  43.0 13.4 %collective-permute-start.2 = (bf16[32,16,256]{2,1,0:T(8,128)(2,1)S(1)}, bf16[32,16,256]{2,1,0:T(8,128)(2,1)S(1)}, u32[]{:S(2)}, u32[]{:S(2)}) collective-permute-start(bf16[32,16,256]{2,1,0:T(8,128)(2,1)S(1)} %get-tuple-element.27), channel_id=1, source_target_pairs={{0,448},{32,480},{64,0},{96,32},{128,64},{160,96},{192,128},{224,1... | collective-permute-start | bytes 786440 | tf_op jit(solution)/shard_map/planes/ppermute | solution.py:591
  58.1 6.8 %collective-permute-start.3 = (bf16[32,16,1536]{2,1,0:T(8,128)(2,1)}, bf16[32,16,1536]{2,1,0:T(8,128)(2,1)}, u32[]{:S(2)}, u32[]{:S(2)}) collective-permute-start(bf16[32,16,1536]{2,1,0:T(8,128)(2,1)} %slice_dynamic-update-slice_fusion.near_in), channel_id=1, source_target_pairs={{0,1},{1,0},{2,3},{3,2},{4,5},{5,4},{6,7},{7,6},{8,9},{9,8},{10,11... | collective-permute-start | bytes 4718600 | tf_op jit(solution)/shard_map/planes/ppermute | solution.py:593
  69.3 30.2 %all-to-all-start.2 = ((f32[32,8,128]{2,1,0:T(8,128)}), f32[32,8,128]{2,1,0:T(8,128)S(1)}, u32[]{:S(2)}, u32[]{:S(2)}) async-start(f32[32,8,128]{2,1,0:T(8,128)} %get-tuple-element.16), calls=%async_computation.2 | async-start | bytes 262144 | tf_op jit(solution)/shard_map/sums/all_to_all | solution.py:598
  83.7 3.8 %collective-permute-start.4 = (bf16[1536,128]{1,0:T(8,128)(2,1)}, bf16[1536,128]{1,0:T(8,128)(2,1)S(1)}, u32[]{:S(2)}, u32[]{:S(2)}) collective-permute-start(bf16[1536,128]{1,0:T(8,128)(2,1)} %get-tuple-element.15.own_in.pair_in), channel_id=1, source_target_pairs={{0,1},{1,0},{2,3},{3,2},{4,5},{5,4},{6,7},{7,6},{8,9},{9,8},{10,11... | collective-permute-start | bytes 1179656 | tf_op jit(solution)/shard_map/items_back/ppermute | solution.py:600
  100.4 12.9 %all-to-all-start.3 = ((bf16[16,16,1152]{2,1,0:T(8,128)(2,1)}), bf16[16,16,1152]{2,1,0:T(8,128)(2,1)S(1)}, u32[]{:S(2)}, u32[]{:S(2)}) async-start(bf16[16,16,1152]{2,1,0:T(8,128)(2,1)} %get-tuple-element.18), calls=%async_computation.3 | async-start | bytes 1179648 | tf_op jit(solution)/shard_map/items_back/all_to_all | solution.py:603
  104.0 9.3 %copy-start = (bf16[16,1024]{1,0:T(8,128)(2,1)S(1)}, bf16[16,1024]{1,0:T(8,128)(2,1)}, u32[]{:S(2)}) copy-start(bf16[16,1024]{1,0:T(8,128)(2,1)} %table_ref.1) | copy-start | bytes 98308
